TPU v7x, 512 devices: a whole 4x8x8 slice. The times are simulated.
512 devices in a mesh: island: 4 (over y_lo), fsdp: 128 (over x, z, y_hi, core).
Axes of the slice: x: 4, y: 8 (y_hi: 2, y_lo: 4; y = y_hi * 4 + y_lo), z: 8, core: 2. Of those that a mesh axis runs over, the one named last changes fastest.
Arguments:
- tokens: bfloat16 [4, 384, 4096], P('island', 'fsdp'), may hold values from -6 to 6
- cotangent: bfloat16 [4, 384, 4096], P('island', 'fsdp'), may hold values from -0.4375 to 0.4375
- w_gate: bfloat16 [14336, 4096], P('fsdp', 'island'), may hold values from -0.09375 to 0.09375
- w_up: bfloat16 [14336, 4096], P('fsdp', 'island'), may hold values from -0.09375 to 0.09375
- down_master: float32 [4, 14336, 4096], P('island', 'fsdp'), may hold values from -3 to 3
- second_moment: float32 [4, 14336], P('island', 'fsdp'), may hold values from 0.3 to 3
- outer_params: float32 [4194304], P('fsdp'), may hold values from -6 to 6
- inner_params: float32 [4, 4194304], P('island', 'fsdp'), may hold values from -6 to 6
- outer_momentum: float32 [4194304], P('fsdp'), may hold values from -3 to 3
Outputs:
- new_down: float32 [4, 14336, 4096], P('island', 'fsdp')
- new_second: float32 [4, 14336], P('island', 'fsdp')
- new_outer: float32 [4194304], P('fsdp')
- new_momentum: float32 [4194304], P('fsdp')
All inputs are finite; a program needn't handle non-finite values.
Results may differ from a plain program's by a relative error of at most 0.0018.
Values may be sent and summed in bfloat16 or wider, within the bound.
No kernel may reach another device: no remote copies, remote signals or barrier semaphores. Data moves between devices by JAX's collectives and lax.ppermute only.
A program may use at most 64 MiB of HBM per device.

v0:
```python
import jax
import jax.numpy as jnp
from jax import lax
from jax.sharding import PartitionSpec as P


def local(
    tokens,
    cotangent,
    w_gate,
    w_up,
    down_master,
    second_moment,
    outer_params,
    inner_params,
    outer_momentum,
):
    gate_full, upward_full = (
        lax.all_gather(w_gate, "island", axis=1, tiled=True),
        lax.all_gather(w_up, "island", axis=1, tiled=True),
    )
    contract = (((1,), (1,)), ((), ()))
    rows_pair = (((0,), (0,)), ((), ()))
    piece = lax.all_gather(tokens[0], "fsdp", axis=0, tiled=True)
    gate = lax.dot_general(piece, gate_full, contract, preferred_element_type=jnp.float32)
    upward = lax.dot_general(piece, upward_full, contract, preferred_element_type=jnp.float32)
    hidden = (jax.nn.silu(gate) * upward).astype(jnp.bfloat16)
    grad = lax.dot_general(
        hidden,
        lax.all_gather(cotangent[0], "fsdp", axis=0, tiled=True),
        rows_pair,
        preferred_element_type=jnp.float32,
    )
    new_second = 0.95 * second_moment[0] + 0.05 * jnp.mean(grad * grad, axis=1)
    new_down = down_master[0] - 0.3 * grad / (jnp.sqrt(new_second)[:, None] + 1e-08)
    difference = outer_params - inner_params[0]
    pseudo = lax.psum(difference, "island") / lax.axis_size("island")
    new_momentum = 0.9 * outer_momentum + pseudo
    new_outer = outer_params - 0.7 * (pseudo + 0.9 * new_momentum)
    return (new_down[None], new_second[None], new_outer, new_momentum)


def solution(mesh):
    placed = (
        P("island", "fsdp", None),
        P("island", "fsdp", None),
        P("fsdp", "island"),
        P("fsdp", "island"),
        P("island", "fsdp", None),
        P("island", "fsdp"),
        P("fsdp"),
        P("island", "fsdp"),
        P("fsdp"),
    )
    return jax.shard_map(
        local,
        mesh=mesh,
        in_specs=placed,
        out_specs=(P("island", "fsdp", None), P("island", "fsdp"), P("fsdp"), P("fsdp")),
        check_vma=False,
    )
```

profile of v0, /device:TPU:1, one launch (start us, length us, event | category | flops | bytes accessed | tf_op | source)
XLA Modules:
  0.0 338.3 jit_solution(8538736712153220928)
XLA Ops:
  8.0 0.0 copy-start.1
  8.0 0.0 copy-start.2
  8.0 0.0 all-reduce.2.cloned.1.call-start
  8.1 1.7 sub.10
  9.8 0.0 all-reduce.2.cloned.1.call-update
  9.8 0.0 all-gather.5.cloned.1.call-start
  9.8 1.4 copy.15
  11.3 0.0 all-gather.5.cloned.1.call-update
  11.3 0.0 all-gather.7.cloned.1.call-start
  11.3 1.4 copy.16
  12.8 0.0 all-gather.7.cloned.1.call-update
  12.8 18.5 %all_gather.13 = bf16[112,4096]{1,0:T(8,128)(2,1)S(1)} all-gather(bf16[112,1024]{1,0:T(8,128)(2,1)} %param.11), channel_id=1, replica_groups=mesh['island'=4,'fsdp'=128] {'island'}, dimensions={1}, use_global_device_ids=true | all-gather | bytes 1146880 | tf_op jit(solution)/shard_map/all_gather | solution.py:19
  31.3 18.6 %all_gather.14 = bf16[112,4096]{1,0:T(8,128)(2,1)S(1)} all-gather(bf16[112,1024]{1,0:T(8,128)(2,1)} %param.12), channel_id=1, replica_groups=mesh['island'=4,'fsdp'=128] {'island'}, dimensions={1}, use_global_device_ids=true | all-gather | bytes 1146880 | tf_op jit(solution)/shard_map/all_gather | solution.py:20
  49.9 20.2 %all-reduce.2.cloned.1.call-done = f32[32768]{0:T(1024)} async-done(((f32[32768]{0:T(1024)}), f32[32768]{0:T(1024)}) %all-reduce.2.cloned.1.call-update) | async-done | bytes 131088 | tf_op jit(solution)/shard_map/psum | solution.py:37
  70.1 0.0 copy-done.1
  70.1 0.0 copy-done.2
  70.1 1.6 multiply_subtract_fusion
  71.7 96.6 %all-gather.5.cloned.1.call-done = bf16[1,384,4096]{2,0,1:T(2,128)(2,1)} async-done(((bf16[1,3,4096]{2,0,1:T(2,128)(2,1)}), bf16[1,384,4096]{2,0,1:T(2,128)(2,1)}) %all-gather.5.cloned.1.call-update) | async-done | bytes 3145744 | tf_op jit(solution)/shard_map/all_gather | solution.py:24
  168.3 6.4 %fusion.5 = f32[384,112]{0,1:T(8,128)S(1)} fusion(bf16[112,4096]{1,0:T(8,128)(2,1)S(1)} %all_gather.13, bf16[1,384,4096]{2,0,1:T(2,128)(2,1)} %all-gather.5.cloned.1.call-done), kind=kOutput, calls=%fused_computation.5 | convolution fusion | flops 352321536 | bytes 4235264 | tf_op jit(solution)/shard_map/dot_general | solution.py:25
  174.7 0.0 copy-start.3
  174.7 0.0 copy-start
  174.7 139.5 %all-gather.7.cloned.1.call-done = bf16[1,384,4096]{2,0,1:T(2,128)(2,1)} async-done(((bf16[1,3,4096]{2,0,1:T(2,128)(2,1)}), bf16[1,384,4096]{2,0,1:T(2,128)(2,1)}) %all-gather.7.cloned.1.call-update) | async-done | bytes 3145744 | tf_op jit(solution)/shard_map/all_gather | solution.py:30
  314.2 13.1 %multiply_reduce_fusion = (f32[112]{0:T(128)S(1)}, f32[112,4096]{1,0:T(8,128)}) fusion(bf16[1,384,4096]{2,0,1:T(2,128)(2,1)} %all-gather.7.cloned.1.call-done, bf16[112,4096]{1,0:T(8,128)(2,1)S(1)} %all_gather.14, bf16[1,384,4096]{2,0,1:T(2,128)(2,1)} %all-gather.5.cloned.1.call-done, f32[384,112]{0,1:T(8,128)S(1)} %fusion.5), kind=kOutput, calls=%fused_computation.9 | convolution fusion | flops 705818496 | bytes 9216448 | tf_op jit(solution)/shard_map/dot_general | solution.py:28
  327.3 0.0 copy-done.3
  327.3 0.5 bitcast_add_fusion
  327.8 0.0 copy-done
  327.8 3.0 fusion.7
  (1 shorter events, 0.0 us)
Async XLA Ops:
  8.0 62.1 %copy-start.1 = (f32[32768]{0:T(1024)S(1)}, f32[32768]{0:T(1024)}, u32[]{:S(2)}) copy-start(f32[32768]{0:T(1024)} %param.15) | copy-start | bytes 393220
  8.0 62.1 %copy-start.2 = (f32[32768]{0:T(1024)S(1)}, f32[32768]{0:T(1024)}, u32[]{:S(2)}) copy-start(f32[32768]{0:T(1024)} %param.17) | copy-start | bytes 393220
  8.0 62.0 %all-reduce.2.cloned.1.call-start = ((), (), s32[]{:S(2)}) async-start(), calls=%async_computation | async-start | bytes 262144 | tf_op jit(solution)/shard_map/psum | solution.py:37
  9.8 158.5 %all-gather.5.cloned.1.call-start = ((), (), s32[]{:S(2)}) async-start(), calls=%async_computation.1 | async-start | bytes 6340608 | tf_op jit(solution)/shard_map/all_gather | solution.py:24
  11.3 302.9 %all-gather.7.cloned.1.call-start = ((), (), s32[]{:S(2)}) async-start(), calls=%async_computation.2 | async-start | bytes 6340608 | tf_op jit(solution)/shard_map/all_gather | solution.py:30
  174.7 152.6 %copy-start.3 = (f32[1,112]{1,0:T(1,128)S(1)}, f32[1,112]{1,0:T(1,128)}, u32[]{:S(2)}) copy-start(f32[1,112]{1,0:T(1,128)} %param.14) | copy-start | bytes 1348
  174.7 153.1 %copy-start = (f32[1,112,4096]{2,1,0:T(8,128)S(1)}, f32[1,112,4096]{2,1,0:T(8,128)}, u32[]{:S(2)}) copy-start(f32[1,112,4096]{2,1,0:T(8,128)} %param.13) | copy-start | bytes 5505028
Sparse Core Ops, SparseCore 0:
  12.3 57.6 all-reduce.1
Sparse Core Ops, SparseCore 1:
  15.0 153.3 all-gather.4
  173.5 140.6 all-gather.6
where the time goes:
time: 339 us; the launch traced here: 338 us
  waiting for transfers between devices  256 us (76%)
  blocking collectives  37.1 us (11%)
  matrix products  19.4 us (6%)
  between operations  15.5 us (5%)
  other arithmetic  6.88 us (2%)
    all_gather x1, waiting for transfers between devices, local(): lax.all_gather(cotangent[0], 'fsdp', axis=0, tiled=True)  139 us
    all_gather x1, waiting for transfers between devices, local(): piece = lax.all_gather(tokens[0], 'fsdp', axis=0, tiled=True)  96.6 us
    psum x1, waiting for transfers between devices, local(): pseudo = lax.psum(difference, 'island') / lax.axis_size('island')  20.2 us
    all_gather x1, blocking collectives, local(): lax.all_gather(w_up, 'island', axis=1, tiled=True)  18.6 us
    all_gather x1, blocking collectives, local(): lax.all_gather(w_gate, 'island', axis=1, tiled=True)  18.5 us
    dot_general x1, matrix products, local(): lax.dot_general(hidden, lax.all_gather(cotangent[0], 'fsdp', axis=0, tile...  13.1 us
  transfers between devices with their start and end apart: 3, of which 3 were waited for; matrix products, arithmetic and copies ran while one was open for 3% of the time, Pallas kernels for 0%

commit v1 on v0

v1 whole, which is shorter than its diff:
```python
import functools

import jax
import jax.numpy as jnp
import numpy as np
from jax import lax
from jax.experimental import pallas as pl
from jax.experimental.pallas import tpu as pltpu
from jax.sharding import PartitionSpec as P

NX, NZ = 4, 8
BF = jnp.bfloat16
F32 = jnp.float32
ROWS_BY_ROWS = (((1,), (1,)), ((), ()))


def flat(x, z, h, c):
    return (((x % NX) * NZ + z % NZ) * 2 + h) * 2 + c


def pairs(target):
    return [
        (flat(x, z, h, c), flat(*target(x, z, h, c)))
        for x in range(NX)
        for z in range(NZ)
        for h in range(2)
        for c in range(2)
    ]


SWAP = pairs(lambda x, z, h, c: (x, z, h, 1 - c))
HALF = pairs(lambda x, z, h, c: (x, z, 1 - h, c))
EARLY = (
    pairs(lambda x, z, h, c: (x, z ^ 4, h, c)),
    pairs(lambda x, z, h, c: (x, z ^ 2, h, c) if c else (x ^ 2, z, h, c)),
    pairs(lambda x, z, h, c: (x, z ^ 1, h, c) if c else (x ^ 1, z, h, c)),
)
UP = pairs(lambda x, z, h, c: (x + 1, z, h, c) if c else (x, z + 1, h, c))
DOWN = pairs(lambda x, z, h, c: (x - 1, z, h, c) if c else (x, z - 1, h, c))


def row_tables():
    row = np.arange(96)
    e3, e2, e1, half, core, r = (row // 48, row // 24 % 2, row // 12 % 2, row // 6 % 2, row // 3 % 2, row % 3)
    ring = np.concatenate([np.zeros(96), -np.ones(96), np.ones(96), np.where(row < 48, -2, 2)]).astype(np.int32)
    four = lambda v: np.tile(v, 4).astype(np.int32)
    return ring, four(e3), four(e2), four(e1), four(half), four(core), four(r)


def row_ids(me):
    ring, e3, e2, e1, half, core, r = (jnp.asarray(t) for t in row_tables())
    x, z, h = me // 32, me // 4 % 8, me // 2 % 2
    h = h ^ half
    zt = ((z + ring) & 7) ^ (4 * e1)
    xt = x ^ (2 * e2) ^ e3
    zc = z ^ (4 * e1) ^ (2 * e2) ^ e3
    xc = (x + ring) & 3
    tokens = (((xt * 8 + zt) * 2 + h) * 2 + core) * 3 + r
    cots = (((xc * 8 + zc) * 2 + h) * 2 + (1 - core)) * 3 + r
    return tokens[None, :], cots[:, None]


def block_kernel(core_ref, idt_ref, idc_ref, w_ref, dm_ref, sm_ref, *refs):
    own, oth, (nd_ref, ns_ref, hid) = refs[:4], refs[4:8], refs[8:]

    def body(toks, cots):
        for b, tok in enumerate(toks):
            gate, up = None, None
            for j in range(4):
                piece = tok[:, j * 1024 : (j + 1) * 1024]
                g = lax.dot_general(piece, w_ref[j, 0], ROWS_BY_ROWS, preferred_element_type=F32)
                u = lax.dot_general(piece, w_ref[j, 1], ROWS_BY_ROWS, preferred_element_type=F32)
                gate, up = (g, u) if gate is None else (gate + g, up + u)
            hid[b * 96 : (b + 1) * 96, :] = (gate / (1.0 + jnp.exp(-gate)) * up).astype(BF)
        turned = []
        for b in range(4):
            pick = (idc_ref[b * 96 : (b + 1) * 96, :] == idt_ref[...]).astype(F32).astype(BF)
            turned.append(
                lax.dot_general(hid[...], pick, (((0,), (1,)), ((), ())), preferred_element_type=F32).astype(BF)
            )
        total = jnp.zeros((112, 1), F32)
        step = 512
        for d in range(0, 4096, step):
            grad = None
            for b in range(4):
                part = jnp.dot(turned[b], cots[b][:, d : d + step], preferred_element_type=F32)
                grad = part if grad is None else grad + part
            nd_ref[:, d : d + step] = grad
            total = total + jnp.sum(grad * grad, axis=1, keepdims=True)
        second = 0.95 * sm_ref[...] + 0.05 * (total * (1.0 / 4096.0))
        ns_ref[...] = second
        scale = 0.3 / (jnp.sqrt(second) + 1e-08)
        for d in range(0, 4096, step):
            nd_ref[:, d : d + step] = dm_ref[:, d : d + step] - nd_ref[:, d : d + step] * scale

    @pl.when(core_ref[0] == 0)
    def _():
        body(own, oth)

    @pl.when(core_ref[0] == 1)
    def _():
        body(oth, own)


def local(
    tokens,
    cotangent,
    w_gate,
    w_up,
    down_master,
    second_moment,
    outer_params,
    inner_params,
    outer_momentum,
):
    me = lax.axis_index("fsdp")
    core = me % 2
    move = functools.partial(lax.ppermute, axis_name="fsdp")

    weights = lax.all_gather(jnp.stack([w_gate, w_up]), "island", axis=0, tiled=False)
    difference = outer_params - inner_params[0]
    total = lax.psum(difference, "island")

    tok, cot = tokens.reshape(96, 128), cotangent.reshape(96, 128)
    mine = jnp.where(core == 0, tok, cot)
    give = jnp.where(core == 0, cot, tok)
    data = jnp.concatenate([mine, move(give, perm=SWAP)], axis=0)
    data = jnp.concatenate([data, move(data, perm=HALF)], axis=0)
    data = jnp.concatenate([data, move(data, perm=EARLY[0])], axis=0)
    data = jnp.concatenate([data, move(data, perm=EARLY[1])], axis=0)
    data = data.reshape(48, 4096)
    data = jnp.concatenate([data, move(data, perm=EARLY[2])], axis=0)
    below, above = move(data, perm=UP), move(data, perm=DOWN)
    far = jnp.concatenate([move(below[:48], perm=UP), move(above[48:], perm=DOWN)], axis=0)
    own = (data, below, above, far)
    oth = tuple(move(v, perm=SWAP) for v in own)

    idt, idc = row_ids(me)
    vmem = pl.BlockSpec(memory_space=pltpu.VMEM)
    new_down, new_second = pl.pallas_call(
        block_kernel,
        out_shape=(jax.ShapeDtypeStruct((112, 4096), F32), jax.ShapeDtypeStruct((112, 1), F32)),
        in_specs=[pl.BlockSpec(memory_space=pltpu.SMEM)] + [vmem] * 13,
        out_specs=(vmem, vmem),
        scratch_shapes=[pltpu.VMEM((384, 112), BF)],
        compiler_params=pltpu.CompilerParams(vmem_limit_bytes=40 * 2**20),
        cost_estimate=pl.CostEstimate(flops=1_200_000_000, bytes_accessed=12_000_000, transcendentals=43008),
    )(core[None], idt, idc, weights, down_master[0], second_moment[0][:, None], *own, *oth)

    pseudo = total / lax.axis_size("island")
    new_momentum = 0.9 * outer_momentum + pseudo
    new_outer = outer_params - 0.7 * (pseudo + 0.9 * new_momentum)
    return (new_down[None], new_second[:, 0][None], new_outer, new_momentum)


def solution(mesh):
    placed = (
        P("island", "fsdp", None),
        P("island", "fsdp", None),
        P("fsdp", "island"),
        P("fsdp", "island"),
        P("island", "fsdp", None),
        P("island", "fsdp"),
        P("fsdp"),
        P("island", "fsdp"),
        P("fsdp"),
    )
    return jax.shard_map(
        local,
        mesh=mesh,
        in_specs=placed,
        out_specs=(P("island", "fsdp", None), P("island", "fsdp"), P("fsdp"), P("fsdp")),
        check_vma=False,
    )
```

time: 339 us -> 184 us (0.54)
  waiting for transfers between devices: 256 us -> 99.8 us
  starting transfers between devices: 0.13 us -> 48.4 us
  blocking collectives: 37.1 us -> 0 us
  matrix products: 19.4 us -> 0 us
  Pallas kernels: 0 us -> 7.24 us
  local copies, waits for them, and re-layouts: 2.86 us -> 8.73 us
    all_gather x2 -> x1, waiting for transfers between devices: 236 us -> 50 us  [local(): lax.all_gather(jnp.stack([w_gate, w_up]), 'island', axis=0, tiled=False)]
    ppermute x0 -> x13, starting transfers between devices: none -> 48.3 us  [the longest x4 14.5 us: local(): oth = tuple((move(v, perm=SWAP) for v in own))]
    all_gather x2 -> x0, blocking collectives: 37.1 us -> none  [the longest x1 18.6 us: local(): lax.all_gather(w_up, 'island', axis=1, tiled=True)]
    ppermute x0 -> x13, waiting for transfers between devices: none -> 29.8 us  [the longest x1 6.62 us: local(): data = jnp.concatenate([data, move(data, perm=HALF)], axis=0)]
    dot_general x2 -> x0, matrix products: 19.4 us -> none  [the longest x1 13.1 us: local(): lax.dot_general(hidden, lax.all_gather(cotangent[0], 'fsdp', axis=0, tile...]
    pallas_call x0 -> x1, Pallas kernels: none -> 7.24 us  [local(): pl.pallas_call(block_kernel, out_shape=(jax.ShapeDtypeStruct((112, 4096),...]
  transfers between devices with their start and end apart: 3 -> 15, of which waited for: 3 -> 8; matrix products, arithmetic and copies ran while one was open for 3% -> 5% of each run, Pallas kernels for 0% -> 0%
where the time goes in v1:
time: 184 us; the launch traced here: 183 us
  waiting for transfers between devices  99.8 us (54%)
  starting transfers between devices  48.4 us (26%)
  between operations  14.5 us (8%)
  local copies, waits for them, and re-layouts  8.73 us (5%)
  Pallas kernels  7.24 us (4%)
  other arithmetic  4.72 us (3%)
    all_gather x1, waiting for transfers between devices, local(): lax.all_gather(jnp.stack([w_gate, w_up]), 'island', axis=0, tiled=False)  50 us
    psum x1, waiting for transfers between devices, local(): total = lax.psum(difference, 'island')  19.9 us
    ppermute x4, starting transfers between devices, local(): oth = tuple((move(v, perm=SWAP) for v in own))  14.5 us
    ppermute x1, starting transfers between devices, local(): data = jnp.concatenate([mine, move(give, perm=SWAP)], axis=0)  8.79 us
    pallas_call x1, Pallas kernels, local(): pl.pallas_call(block_kernel, out_shape=(jax.ShapeDtypeStruct((112, 4096),...  7.24 us
    ppermute x1, waiting for transfers between devices, local(): data = jnp.concatenate([data, move(data, perm=HALF)], axis=0)  6.62 us
    ppermute x2, starting transfers between devices, local(): below, above = (move(data, perm=UP), move(data, perm=DOWN))  6.59 us
    ppermute x2, waiting for transfers between devices, local(): below, above = (move(data, perm=UP), move(data, perm=DOWN))  6.33 us
  transfers between devices with their start and end apart: 15, of which 8 were waited for; matrix products, arithmetic and copies ran while one was open for 5% of the time, Pallas kernels for 0%

profile of v1, /device:TPU:1, one launch (start us, length us, event | category | flops | bytes accessed | tf_op | source)
XLA Modules:
  0.0 183.3 jit_solution(10799725625094871275)
XLA Ops:
  7.2 0.8 broadcast_select_fusion
  8.1 8.8 %collective-permute-start = (bf16[96,128]{1,0:T(8,128)(2,1)S(1)}, bf16[96,128]{1,0:T(8,128)(2,1)S(1)}, u32[]{:S(2)}, u32[]{:S(2)}) collective-permute-start(bf16[96,128]{1,0:T(8,128)(2,1)S(1)} %select_n.53), channel_id=1, source_target_pairs={{0,1},{1,0},{2,3},{3,2},{4,5},{5,4},{6,7},{7,6},{8,9},{9,8},{10,11... | collective-permute-start | bytes 73736 | tf_op jit(solution)/shard_map/ppermute | solution.py:127
  17.7 2.1 %collective-permute-start.1 = (bf16[192,128]{1,0:T(8,128)(2,1)S(1)}, bf16[192,128]{1,0:T(8,128)(2,1)S(1)}, u32[]{:S(2)}, u32[]{:S(2)}) collective-permute-start(bf16[192,128]{1,0:T(8,128)(2,1)S(1)} %pad_maximum_fusion.3), channel_id=1, source_target_pairs={{0,2},{1,3},{2,0},{3,1},{4,6},{5,7},{6,4},{7,5},{8,10},{9,11},{10,... | collective-permute-start | bytes 147464 | tf_op jit(solution)/shard_map/ppermute | solution.py:128
  19.8 6.6 %collective-permute-done.1 = bf16[192,128]{1,0:T(8,128)(2,1)S(1)} collective-permute-done((bf16[192,128]{1,0:T(8,128)(2,1)S(1)}, bf16[192,128]{1,0:T(8,128)(2,1)S(1)}, u32[]{:S(2)}, u32[]{:S(2)}) %collective-permute-start.1) | collective-permute-done | bytes 49184 | tf_op jit(solution)/shard_map/ppermute | solution.py:128
  26.5 5.5 %collective-permute-start.2 = (bf16[384,128]{1,0:T(8,128)(2,1)S(1)}, bf16[384,128]{1,0:T(8,128)(2,1)S(1)}, u32[]{:S(2)}, u32[]{:S(2)}) collective-permute-start(bf16[384,128]{1,0:T(8,128)(2,1)S(1)} %pad_maximum_fusion.2), channel_id=1, source_target_pairs={{0,16},{1,17},{2,18},{3,19},{4,20},{5,21},{6,22},{7,23},{8,24},{9,... | collective-permute-start | bytes 294920 | tf_op jit(solution)/shard_map/ppermute | solution.py:129
  32.0 3.8 %collective-permute-done.2 = bf16[384,128]{1,0:T(8,128)(2,1)S(1)} collective-permute-done((bf16[384,128]{1,0:T(8,128)(2,1)S(1)}, bf16[384,128]{1,0:T(8,128)(2,1)S(1)}, u32[]{:S(2)}, u32[]{:S(2)}) %collective-permute-start.2) | collective-permute-done | bytes 98336 | tf_op jit(solution)/shard_map/ppermute | solution.py:129
  35.9 2.4 %collective-permute-start.3 = (bf16[768,128]{1,0:T(8,128)(2,1)S(1)}, bf16[768,128]{1,0:T(8,128)(2,1)S(1)}, u32[]{:S(2)}, u32[]{:S(2)}) collective-permute-start(bf16[768,128]{1,0:T(8,128)(2,1)S(1)} %pad_maximum_fusion.1), channel_id=1, source_target_pairs={{0,64},{1,9},{2,66},{3,11},{4,68},{5,13},{6,70},{7,15},{8,72},{9,1... | collective-permute-start | bytes 589832 | tf_op jit(solution)/shard_map/ppermute | solution.py:130
  38.3 6.2 %collective-permute-done.3 = bf16[768,128]{1,0:T(8,128)(2,1)S(1)} collective-permute-done((bf16[768,128]{1,0:T(8,128)(2,1)S(1)}, bf16[768,128]{1,0:T(8,128)(2,1)S(1)}, u32[]{:S(2)}, u32[]{:S(2)}) %collective-permute-start.3) | collective-permute-done | bytes 196640 | tf_op jit(solution)/shard_map/ppermute | solution.py:130
  44.7 1.9 %collective-permute-start.4 = (bf16[48,4096]{1,0:T(8,128)(2,1)S(1)}, bf16[48,4096]{1,0:T(8,128)(2,1)S(1)}, u32[]{:S(2)}, u32[]{:S(2)}) collective-permute-start(bf16[48,4096]{1,0:T(8,128)(2,1)S(1)} %reshape.17), channel_id=1, source_target_pairs={{0,32},{1,5},{2,34},{3,7},{4,36},{5,1},{6,38},{7,3},{8,40},{9,13},... | collective-permute-start | bytes 1179656 | tf_op jit(solution)/shard_map/ppermute | solution.py:132
  46.6 0.8 constant_dynamic-update-slice_fusion.6
  47.4 6.0 %collective-permute-done.4 = bf16[48,4096]{1,0:T(8,128)(2,1)S(1)} collective-permute-done((bf16[48,4096]{1,0:T(8,128)(2,1)S(1)}, bf16[48,4096]{1,0:T(8,128)(2,1)S(1)}, u32[]{:S(2)}, u32[]{:S(2)}) %collective-permute-start.4) | collective-permute-done | bytes 393248 | tf_op jit(solution)/shard_map/ppermute | solution.py:132
  53.5 0.8 constant_dynamic-update-slice_fusion.5.refs_0_
  54.3 3.4 %collective-permute-start.5 = (bf16[96,4096]{1,0:T(8,128)(2,1)}, bf16[96,4096]{1,0:T(8,128)(2,1)S(1)}, u32[]{:S(2)}, u32[]{:S(2)}) collective-permute-start(bf16[96,4096]{1,0:T(8,128)(2,1)} %constant_dynamic-update-slice_fusion.5.refs_0_), channel_id=1, source_target_pairs={{0,4},{1,33},{2,6},{3,35},{4,8},{5,37},{6,10},{7,39},{8,12},{9,41}... | collective-permute-start | bytes 2359304 | tf_op jit(solution)/shard_map/ppermute | solution.py:133
  58.5 0.8 pad_maximum_fusion
  59.3 3.2 %collective-permute-start.6 = (bf16[96,4096]{1,0:T(8,128)(2,1)}, bf16[96,4096]{1,0:T(8,128)(2,1)S(1)}, u32[]{:S(2)}, u32[]{:S(2)}) collective-permute-start(bf16[96,4096]{1,0:T(8,128)(2,1)} %constant_dynamic-update-slice_fusion.5.refs_0_), channel_id=1, source_target_pairs={{0,28},{1,97},{2,30},{3,99},{4,0},{5,101},{6,2},{7,103},{8,4},{9,1... | collective-permute-start | bytes 2359304 | tf_op jit(solution)/shard_map/ppermute | solution.py:133
  62.5 6.3 %collective-permute-done.5.refs_1_ = bf16[96,4096]{1,0:T(8,128)(2,1)S(1)} collective-permute-done((bf16[96,4096]{1,0:T(8,128)(2,1)}, bf16[96,4096]{1,0:T(8,128)(2,1)S(1)}, u32[]{:S(2)}, u32[]{:S(2)}) %collective-permute-start.5) | collective-permute-done | bytes 786464 | tf_op jit(solution)/shard_map/ppermute | solution.py:133
  68.8 0.8 slice.8
  69.6 2.2 %collective-permute-start.7 = (bf16[48,4096]{1,0:T(8,128)(2,1)}, bf16[48,4096]{1,0:T(8,128)(2,1)}, u32[]{:S(2)}, u32[]{:S(2)}) collective-permute-start(bf16[48,4096]{1,0:T(8,128)(2,1)} %slice.8), channel_id=1, source_target_pairs={{0,4},{1,33},{2,6},{3,35},{4,8},{5,37},{6,10},{7,39},{8,12},{9,41}... | collective-permute-start | bytes 1179656 | tf_op jit(solution)/shard_map/ppermute | solution.py:134
  72.0 0.8 broadcast_in_dim.16.idc_ref
  72.9 7.5 %collective-permute-start.9 = (bf16[96,4096]{1,0:T(8,128)(2,1)}, bf16[96,4096]{1,0:T(8,128)(2,1)}, u32[]{:S(2)}, u32[]{:S(2)}) collective-permute-start(bf16[96,4096]{1,0:T(8,128)(2,1)} %constant_dynamic-update-slice_fusion.5.refs_0_), channel_id=1, source_target_pairs={{0,1},{1,0},{2,3},{3,2},{4,5},{5,4},{6,7},{7,6},{8,9},{9,8},{10,11... | collective-permute-start | bytes 2359304 | tf_op jit(solution)/shard_map/ppermute | solution.py:136
  80.5 4.4 %collective-permute-start.8 = (bf16[48,4096]{1,0:T(8,128)(2,1)S(1)}, bf16[48,4096]{1,0:T(8,128)(2,1)S(1)}, u32[]{:S(2)}, u32[]{:S(2)}) collective-permute-start(bf16[48,4096]{1,0:T(8,128)(2,1)S(1)} %slice.9), channel_id=1, source_target_pairs={{0,28},{1,97},{2,30},{3,99},{4,0},{5,101},{6,2},{7,103},{8,4},{9,1... | collective-permute-start | bytes 1179656 | tf_op jit(solution)/shard_map/ppermute | solution.py:134
  84.8 2.7 %collective-permute-start.10 = (bf16[96,4096]{1,0:T(8,128)(2,1)S(1)}, bf16[96,4096]{1,0:T(8,128)(2,1)}, u32[]{:S(2)}, u32[]{:S(2)}) collective-permute-start(bf16[96,4096]{1,0:T(8,128)(2,1)S(1)} %collective-permute-done.5.refs_1_), channel_id=1, source_target_pairs={{0,1},{1,0},{2,3},{3,2},{4,5},{5,4},{6,7},{7,6},{8,9},{9,8},{10,11... | collective-permute-start | bytes 2359304 | tf_op jit(solution)/shard_map/ppermute | solution.py:136
  87.5 1.9 %collective-permute-start.11 = (bf16[96,4096]{1,0:T(8,128)(2,1)S(1)}, bf16[96,4096]{1,0:T(8,128)(2,1)}, u32[]{:S(2)}, u32[]{:S(2)}) collective-permute-start(bf16[96,4096]{1,0:T(8,128)(2,1)S(1)} %collective-permute-done.6.refs_2_), channel_id=1, source_target_pairs={{0,1},{1,0},{2,3},{3,2},{4,5},{5,4},{6,7},{7,6},{8,9},{9,8},{10,11... | collective-permute-start | bytes 2359304 | tf_op jit(solution)/shard_map/ppermute | solution.py:136
  89.5 1.8 constant_dynamic-update-slice_fusion.8
  91.3 0.8 constant_dynamic-update-slice_fusion.7.refs_3_
  92.1 2.4 %collective-permute-start.12 = (bf16[96,4096]{1,0:T(8,128)(2,1)}, bf16[96,4096]{1,0:T(8,128)(2,1)}, u32[]{:S(2)}, u32[]{:S(2)}) collective-permute-start(bf16[96,4096]{1,0:T(8,128)(2,1)} %constant_dynamic-update-slice_fusion.7.refs_3_), channel_id=1, source_target_pairs={{0,1},{1,0},{2,3},{3,2},{4,5},{5,4},{6,7},{7,6},{8,9},{9,8},{10,11... | collective-permute-start | bytes 2359304 | tf_op jit(solution)/shard_map/ppermute | solution.py:136
  94.5 19.9 %all-reduce.2.cloned.1.call-done = f32[32768]{0:T(1024)} async-done(((f32[32768]{0:T(1024)}), f32[32768]{0:T(1024)}) %all-reduce.2.cloned.1.call-update) | async-done | bytes 131088 | tf_op jit(solution)/shard_map/psum | solution.py:122
  114.4 1.8 multiply_subtract_fusion
  116.2 50.0 %all-gather.3.cloned.1.call-done = bf16[8,112,1024]{2,1,0:T(8,128)(2,1)} async-done(((bf16[2,112,1024]{2,1,0:T(8,128)(2,1)}), bf16[8,112,1024]{2,1,0:T(8,128)(2,1)}) %all-gather.3.cloned.1.call-update) | async-done | bytes 1835024 | tf_op jit(solution)/shard_map/all_gather | solution.py:120
  166.2 1.5 copy-done.1
  167.7 0.9 copy-done.2
  168.6 7.2 %shard_map.183 = (f32[112,4096]{1,0:T(8,128)}, f32[112,1]{1,0:T(8,128)S(1)}) custom-call(s32[1]{0:T(128)} %bitcast.core_ref, s32[1,384]{1,0:T(1,128)S(1)} %broadcast_in_dim.13.idt_ref, s32[384,1]{1,0:T(8,128)S(1)} %copy-done.2, bf16[4,2,112,1024]{3,2,1,0:T(8,128)(2,1)S(1)} %bitcast.10, f32[112,4096]{1,0:T(8,128)S(1)} %bitcast.9, f32[112,1]{1,0:T(8,128)S(1)} %copy.24.sm_ref, ...), custom_call_target="tpu_custom_call" | custom-call | flops 1200000000 | bytes 12000000 | tf_op jit(solution)/shard_map/pallas_call | solution.py:140
  (59 shorter events, 2.8 us)
Async XLA Ops:
  7.2 107.2 %all-reduce.2.cloned.1.call-start = ((), (), s32[]{:S(2)}) async-start(), calls=%async_computation | async-start | bytes 262144 | tf_op jit(solution)/shard_map/psum | solution.py:122
  8.1 9.6 %collective-permute-start = (bf16[96,128]{1,0:T(8,128)(2,1)S(1)}, bf16[96,128]{1,0:T(8,128)(2,1)S(1)}, u32[]{:S(2)}, u32[]{:S(2)}) collective-permute-start(bf16[96,128]{1,0:T(8,128)(2,1)S(1)} %select_n.53), channel_id=1, source_target_pairs={{0,1},{1,0},{2,3},{3,2},{4,5},{5,4},{6,7},{7,6},{8,9},{9,8},{10,11... | collective-permute-start | bytes 73736 | tf_op jit(solution)/shard_map/ppermute | solution.py:127
  17.7 8.7 %collective-permute-start.1 = (bf16[192,128]{1,0:T(8,128)(2,1)S(1)}, bf16[192,128]{1,0:T(8,128)(2,1)S(1)}, u32[]{:S(2)}, u32[]{:S(2)}) collective-permute-start(bf16[192,128]{1,0:T(8,128)(2,1)S(1)} %pad_maximum_fusion.3), channel_id=1, source_target_pairs={{0,2},{1,3},{2,0},{3,1},{4,6},{5,7},{6,4},{7,5},{8,10},{9,11},{10,... | collective-permute-start | bytes 147464 | tf_op jit(solution)/shard_map/ppermute | solution.py:128
  19.8 37.9 %copy-start.3 = (f32[32768]{0:T(1024)S(1)}, f32[32768]{0:T(1024)}, u32[]{:S(2)}) copy-start(f32[32768]{0:T(1024)} %param.22) | copy-start | bytes 393220
  19.8 37.9 %copy-start.6 = (f32[1,32768]{1,0:T(1,128)S(1)}, f32[1,32768]{1,0:T(1,128)}, u32[]{:S(2)}) copy-start(f32[1,32768]{1,0:T(1,128)} %param.23) | copy-start | bytes 393220
  26.5 9.4 %collective-permute-start.2 = (bf16[384,128]{1,0:T(8,128)(2,1)S(1)}, bf16[384,128]{1,0:T(8,128)(2,1)S(1)}, u32[]{:S(2)}, u32[]{:S(2)}) collective-permute-start(bf16[384,128]{1,0:T(8,128)(2,1)S(1)} %pad_maximum_fusion.2), channel_id=1, source_target_pairs={{0,16},{1,17},{2,18},{3,19},{4,20},{5,21},{6,22},{7,23},{8,24},{9,... | collective-permute-start | bytes 294920 | tf_op jit(solution)/shard_map/ppermute | solution.py:129
  35.8 22.6 %copy-start.4 = (bf16[112,1024]{1,0:T(8,128)(2,1)S(1)}, bf16[112,1024]{1,0:T(8,128)(2,1)}, u32[]{:S(2)}) copy-start(bf16[112,1024]{1,0:T(8,128)(2,1)} %param.19) | copy-start | bytes 688132
  35.8 22.6 %copy-start.5 = (bf16[112,1024]{1,0:T(8,128)(2,1)S(1)}, bf16[112,1024]{1,0:T(8,128)(2,1)}, u32[]{:S(2)}) copy-start(bf16[112,1024]{1,0:T(8,128)(2,1)} %param.18) | copy-start | bytes 688132
  35.9 8.6 %collective-permute-start.3 = (bf16[768,128]{1,0:T(8,128)(2,1)S(1)}, bf16[768,128]{1,0:T(8,128)(2,1)S(1)}, u32[]{:S(2)}, u32[]{:S(2)}) collective-permute-start(bf16[768,128]{1,0:T(8,128)(2,1)S(1)} %pad_maximum_fusion.1), channel_id=1, source_target_pairs={{0,64},{1,9},{2,66},{3,11},{4,68},{5,13},{6,70},{7,15},{8,72},{9,1... | collective-permute-start | bytes 589832 | tf_op jit(solution)/shard_map/ppermute | solution.py:130
  44.7 8.8 %collective-permute-start.4 = (bf16[48,4096]{1,0:T(8,128)(2,1)S(1)}, bf16[48,4096]{1,0:T(8,128)(2,1)S(1)}, u32[]{:S(2)}, u32[]{:S(2)}) collective-permute-start(bf16[48,4096]{1,0:T(8,128)(2,1)S(1)} %reshape.17), channel_id=1, source_target_pairs={{0,32},{1,5},{2,34},{3,7},{4,36},{5,1},{6,38},{7,3},{8,40},{9,13},... | collective-permute-start | bytes 1179656 | tf_op jit(solution)/shard_map/ppermute | solution.py:132
  47.4 24.5 %copy-start.7 = (s32[384]{0:T(512)S(1)}, s32[384]{0:T(512)}, u32[]{:S(2)}) copy-start(s32[384]{0:T(512)} %constant.106) | copy-start | bytes 4612
  47.4 24.5 %copy-start.8 = (s32[384]{0:T(512)S(1)}, s32[384]{0:T(512)}, u32[]{:S(2)}) copy-start(s32[384]{0:T(512)} %constant.107) | copy-start | bytes 4612
  47.4 24.5 %copy-start.9 = (s32[384]{0:T(512)S(1)}, s32[384]{0:T(512)}, u32[]{:S(2)}) copy-start(s32[384]{0:T(512)} %constant.109) | copy-start | bytes 4612
  47.4 24.5 %copy-start.10 = (s32[384]{0:T(512)S(1)}, s32[384]{0:T(512)}, u32[]{:S(2)}) copy-start(s32[384]{0:T(512)} %constant.92.clone) | copy-start | bytes 4612
  47.4 24.5 %copy-start.11 = (s32[384]{0:T(512)S(1)}, s32[384]{0:T(512)}, u32[]{:S(2)}) copy-start(s32[384]{0:T(512)} %constant.93.clone) | copy-start | bytes 4612
  47.4 24.5 %copy-start.12 = (s32[384]{0:T(512)S(1)}, s32[384]{0:T(512)}, u32[]{:S(2)}) copy-start(s32[384]{0:T(512)} %constant.96.clone) | copy-start | bytes 4612
  47.4 24.5 %copy-start.13 = (s32[384]{0:T(512)S(1)}, s32[384]{0:T(512)}, u32[]{:S(2)}) copy-start(s32[384]{0:T(512)} %constant.97.clone) | copy-start | bytes 4612
  47.4 24.5 %copy-start.14 = (s32[384]{0:T(512)S(1)}, s32[384]{0:T(512)}, u32[]{:S(2)}) copy-start(s32[384]{0:T(512)} %constant.98.clone) | copy-start | bytes 4612
  47.4 25.4 %copy-start.15 = (f32[1,112]{1,0:T(1,128)S(1)}, f32[1,112]{1,0:T(1,128)}, u32[]{:S(2)}) copy-start(f32[1,112]{1,0:T(1,128)} %param.21) | copy-start | bytes 1348
  54.3 14.5 %collective-permute-start.5 = (bf16[96,4096]{1,0:T(8,128)(2,1)}, bf16[96,4096]{1,0:T(8,128)(2,1)S(1)}, u32[]{:S(2)}, u32[]{:S(2)}) collective-permute-start(bf16[96,4096]{1,0:T(8,128)(2,1)} %constant_dynamic-update-slice_fusion.5.refs_0_), channel_id=1, source_target_pairs={{0,4},{1,33},{2,6},{3,35},{4,8},{5,37},{6,10},{7,39},{8,12},{9,41}... | collective-permute-start | bytes 2359304 | tf_op jit(solution)/shard_map/ppermute | solution.py:133
  58.4 107.8 %all-gather.3.cloned.1.call-start = ((), (), s32[]{:S(2)}) async-start(), calls=%async_computation.1 | async-start | bytes 2293760 | tf_op jit(solution)/shard_map/all_gather | solution.py:120
  59.3 21.1 %collective-permute-start.6 = (bf16[96,4096]{1,0:T(8,128)(2,1)}, bf16[96,4096]{1,0:T(8,128)(2,1)S(1)}, u32[]{:S(2)}, u32[]{:S(2)}) collective-permute-start(bf16[96,4096]{1,0:T(8,128)(2,1)} %constant_dynamic-update-slice_fusion.5.refs_0_), channel_id=1, source_target_pairs={{0,28},{1,97},{2,30},{3,99},{4,0},{5,101},{6,2},{7,103},{8,4},{9,1... | collective-permute-start | bytes 2359304 | tf_op jit(solution)/shard_map/ppermute | solution.py:133
  69.6 96.6 %copy-start = (f32[1,112,4096]{2,1,0:T(8,128)S(1)}, f32[1,112,4096]{2,1,0:T(8,128)}, u32[]{:S(2)}) copy-start(f32[1,112,4096]{2,1,0:T(8,128)} %param.20) | copy-start | bytes 5505028
  69.6 19.9 %collective-permute-start.7 = (bf16[48,4096]{1,0:T(8,128)(2,1)}, bf16[48,4096]{1,0:T(8,128)(2,1)}, u32[]{:S(2)}, u32[]{:S(2)}) collective-permute-start(bf16[48,4096]{1,0:T(8,128)(2,1)} %slice.8), channel_id=1, source_target_pairs={{0,4},{1,33},{2,6},{3,35},{4,8},{5,37},{6,10},{7,39},{8,12},{9,41}... | collective-permute-start | bytes 1179656 | tf_op jit(solution)/shard_map/ppermute | solution.py:134
  72.9 43.2 %collective-permute-start.9 = (bf16[96,4096]{1,0:T(8,128)(2,1)}, bf16[96,4096]{1,0:T(8,128)(2,1)}, u32[]{:S(2)}, u32[]{:S(2)}) collective-permute-start(bf16[96,4096]{1,0:T(8,128)(2,1)} %constant_dynamic-update-slice_fusion.5.refs_0_), channel_id=1, source_target_pairs={{0,1},{1,0},{2,3},{3,2},{4,5},{5,4},{6,7},{7,6},{8,9},{9,8},{10,11... | collective-permute-start | bytes 2359304 | tf_op jit(solution)/shard_map/ppermute | solution.py:136
  80.5 10.8 %collective-permute-start.8 = (bf16[48,4096]{1,0:T(8,128)(2,1)S(1)}, bf16[48,4096]{1,0:T(8,128)(2,1)S(1)}, u32[]{:S(2)}, u32[]{:S(2)}) collective-permute-start(bf16[48,4096]{1,0:T(8,128)(2,1)S(1)} %slice.9), channel_id=1, source_target_pairs={{0,28},{1,97},{2,30},{3,99},{4,0},{5,101},{6,2},{7,103},{8,4},{9,1... | collective-permute-start | bytes 1179656 | tf_op jit(solution)/shard_map/ppermute | solution.py:134
  84.8 31.3 %collective-permute-start.10 = (bf16[96,4096]{1,0:T(8,128)(2,1)S(1)}, bf16[96,4096]{1,0:T(8,128)(2,1)}, u32[]{:S(2)}, u32[]{:S(2)}) collective-permute-start(bf16[96,4096]{1,0:T(8,128)(2,1)S(1)} %collective-permute-done.5.refs_1_), channel_id=1, source_target_pairs={{0,1},{1,0},{2,3},{3,2},{4,5},{5,4},{6,7},{7,6},{8,9},{9,8},{10,11... | collective-permute-start | bytes 2359304 | tf_op jit(solution)/shard_map/ppermute | solution.py:136
  87.5 28.6 %collective-permute-start.11 = (bf16[96,4096]{1,0:T(8,128)(2,1)S(1)}, bf16[96,4096]{1,0:T(8,128)(2,1)}, u32[]{:S(2)}, u32[]{:S(2)}) collective-permute-start(bf16[96,4096]{1,0:T(8,128)(2,1)S(1)} %collective-permute-done.6.refs_2_), channel_id=1, source_target_pairs={{0,1},{1,0},{2,3},{3,2},{4,5},{5,4},{6,7},{7,6},{8,9},{9,8},{10,11... | collective-permute-start | bytes 2359304 | tf_op jit(solution)/shard_map/ppermute | solution.py:136
  92.1 24.1 %collective-permute-start.12 = (bf16[96,4096]{1,0:T(8,128)(2,1)}, bf16[96,4096]{1,0:T(8,128)(2,1)}, u32[]{:S(2)}, u32[]{:S(2)}) collective-permute-start(bf16[96,4096]{1,0:T(8,128)(2,1)} %constant_dynamic-update-slice_fusion.7.refs_3_), channel_id=1, source_target_pairs={{0,1},{1,0},{2,3},{3,2},{4,5},{5,4},{6,7},{7,6},{8,9},{9,8},{10,11... | collective-permute-start | bytes 2359304 | tf_op jit(solution)/shard_map/ppermute | solution.py:136
  166.2 1.5 copy-start.1
  167.7 0.9 copy-start.2
Sparse Core Ops, SparseCore 0:
  58.5 55.8 all-reduce.1
  117.3 48.8 all-gather.2

commit v2 on v1

--- a/solution.py
+++ b/solution.py
@@ -30,10 +30,9 @@
 
 SWAP = pairs(lambda x, z, h, c: (x, z, h, 1 - c))
 HALF = pairs(lambda x, z, h, c: (x, z, 1 - h, c))
-EARLY = (
-    pairs(lambda x, z, h, c: (x, z ^ 4, h, c)),
-    pairs(lambda x, z, h, c: (x, z ^ 2, h, c) if c else (x ^ 2, z, h, c)),
-    pairs(lambda x, z, h, c: (x, z ^ 1, h, c) if c else (x ^ 1, z, h, c)),
+FAR = pairs(lambda x, z, h, c: (x, z ^ 4, h, c))
+FIRST = tuple(
+    pairs(lambda x, z, h, c, s=s: (x, z + s, h, c) if c else (x + s, z, h, c)) for s in (1, -1, -2)
 )
 UP = pairs(lambda x, z, h, c: (x + 1, z, h, c) if c else (x, z + 1, h, c))
 DOWN = pairs(lambda x, z, h, c: (x - 1, z, h, c) if c else (x, z - 1, h, c))
@@ -41,22 +40,18 @@
 
 def row_tables():
     row = np.arange(96)
-    e3, e2, e1, half, core, r = (row // 48, row // 24 % 2, row // 12 % 2, row // 6 % 2, row // 3 % 2, row % 3)
-    ring = np.concatenate([np.zeros(96), -np.ones(96), np.ones(96), np.where(row < 48, -2, 2)]).astype(np.int32)
-    four = lambda v: np.tile(v, 4).astype(np.int32)
-    return ring, four(e3), four(e2), four(e1), four(half), four(core), four(r)
+    early = np.array([0, -1, 1, 2])[row // 24]
+    ring = np.concatenate([np.zeros(96), -np.ones(96), np.ones(96), np.where(row < 48, -2, 2)])
+    inner = [np.tile(v, 4) for v in (early, row // 12 % 2 * 4, row // 6 % 2, row // 3 % 2, row % 3)]
+    return [jnp.asarray(v.astype(np.int32)) for v in (ring, *inner)]
 
 
 def row_ids(me):
-    ring, e3, e2, e1, half, core, r = (jnp.asarray(t) for t in row_tables())
+    ring, early, four, half, core, r = row_tables()
     x, z, h = me // 32, me // 4 % 8, me // 2 % 2
     h = h ^ half
-    zt = ((z + ring) & 7) ^ (4 * e1)
-    xt = x ^ (2 * e2) ^ e3
-    zc = z ^ (4 * e1) ^ (2 * e2) ^ e3
-    xc = (x + ring) & 3
-    tokens = (((xt * 8 + zt) * 2 + h) * 2 + core) * 3 + r
-    cots = (((xc * 8 + zc) * 2 + h) * 2 + (1 - core)) * 3 + r
+    tokens = (((((x + early) & 3) * 8 + (((z + ring) & 7) ^ four)) * 2 + h) * 2 + core) * 3 + r
+    cots = (((((x + ring) & 3) * 8 + (((z + early) & 7) ^ four)) * 2 + h) * 2 + (1 - core)) * 3 + r
     return tokens[None, :], cots[:, None]
 
 
@@ -119,19 +114,24 @@
 
     weights = lax.all_gather(jnp.stack([w_gate, w_up]), "island", axis=0, tiled=False)
     difference = outer_params - inner_params[0]
-    total = lax.psum(difference, "island")
+    pair = difference + lax.ppermute(difference, "island", ((0, 1), (1, 0), (2, 3), (3, 2)))
+    total = pair + lax.ppermute(pair, "island", ((0, 2), (2, 0), (1, 3), (3, 1)))
 
     tok, cot = tokens.reshape(96, 128), cotangent.reshape(96, 128)
     mine = jnp.where(core == 0, tok, cot)
     give = jnp.where(core == 0, cot, tok)
     data = jnp.concatenate([mine, move(give, perm=SWAP)], axis=0)
     data = jnp.concatenate([data, move(data, perm=HALF)], axis=0)
-    data = jnp.concatenate([data, move(data, perm=EARLY[0])], axis=0)
-    data = jnp.concatenate([data, move(data, perm=EARLY[1])], axis=0)
-    data = data.reshape(48, 4096)
-    data = jnp.concatenate([data, move(data, perm=EARLY[2])], axis=0)
-    below, above = move(data, perm=UP), move(data, perm=DOWN)
-    far = jnp.concatenate([move(below[:48], perm=UP), move(above[48:], perm=DOWN)], axis=0)
+    data = jnp.concatenate([data, move(data, perm=FAR)], axis=0) + (total[0] * 0).astype(BF)
+    data = data.reshape(24, 4096)
+    data = jnp.concatenate([data] + [move(data, perm=p) for p in FIRST], axis=0)
+    lo, hi = data[:48], data[48:]
+    below_lo, above_hi = move(lo, perm=UP), move(hi, perm=DOWN)
+    below_hi, above_lo = move(hi, perm=UP), move(lo, perm=DOWN)
+    tie = weights[0, 0, 0, 0] * 0
+    far = jnp.concatenate([move(below_lo + tie, perm=UP), move(above_hi + tie, perm=DOWN)], axis=0)
+    below = jnp.concatenate([below_lo, below_hi], axis=0)
+    above = jnp.concatenate([above_lo, above_hi], axis=0)
     own = (data, below, above, far)
     oth = tuple(move(v, perm=SWAP) for v in own)
 

time: 184 us -> 120 us (0.65)
  waiting for transfers between devices: 99.8 us -> 8.42 us
  starting transfers between devices: 48.4 us -> 74 us
    all_gather x1, waiting for transfers between devices: 50 us -> 0.02 us  [local(): lax.all_gather(jnp.stack([w_gate, w_up]), 'island', axis=0, tiled=False)]
    ppermute x7 -> x12, starting transfers between devices: 23 us -> 44.7 us  [the longest x3 15.5 us: local(): data = jnp.concatenate([data] + [move(data, perm=p) for p in FIRST], axis=0)]
    psum x1 -> x0, waiting for transfers between devices: 19.9 us -> none  [local(): total = lax.psum(difference, 'island')]
    ppermute x7 -> x12, waiting for transfers between devices: 22.4 us -> 6.47 us  [the longest x3 3.88 us: local(): data = jnp.concatenate([data] + [move(data, perm=p) for p in FIRST], axis=0)]
    ppermute x1, waiting for transfers between devices: 6.62 us -> 0.31 us  [local(): data = jnp.concatenate([data, move(data, perm=HALF)], axis=0)]
    ppermute x4, starting transfers between devices: 14.5 us -> 18.1 us  [local(): oth = tuple((move(v, perm=SWAP) for v in own))]
    unnamed x38 -> x28, local copies, waits for them, and re-layouts: 5.13 us -> 3.2 us
  transfers between devices with their start and end apart: 15 -> 19, of which waited for: 8 -> 4; matrix products, arithmetic and copies ran while one was open for 5% -> 9% of each run, Pallas kernels for 0% -> 0%
where the time goes in v2:
time: 120 us; the launch traced here: 119 us
  starting transfers between devices  74 us (62%)
  between operations  16 us (13%)
  waiting for transfers between devices  8.42 us (7%)
  local copies, waits for them, and re-layouts  7.74 us (6%)
  Pallas kernels  7.33 us (6%)
  other arithmetic  6.02 us (5%)
    ppermute x4, starting transfers between devices, local(): oth = tuple((move(v, perm=SWAP) for v in own))  18.1 us
    ppermute x3, starting transfers between devices, local(): data = jnp.concatenate([data] + [move(data, perm=p) for p in FIRST], axis=0)  15.5 us
    ppermute x1, starting transfers between devices, local(): data = jnp.concatenate([mine, move(give, perm=SWAP)], axis=0)  8.79 us
    ppermute x1, starting transfers between devices, local(): move(data, perm=FAR)  8.31 us
    pallas_call x1, Pallas kernels, local(): pl.pallas_call(block_kernel, out_shape=(jax.ShapeDtypeStruct((112, 4096),...  7.33 us
    ppermute x2, starting transfers between devices, local(): below_hi, above_lo = (move(hi, perm=UP), move(lo, perm=DOWN))  7.04 us
    ppermute x2, starting transfers between devices, local(): below_lo, above_hi = (move(lo, perm=UP), move(hi, perm=DOWN))  4.36 us
    ppermute x3, waiting for transfers between devices, local(): data = jnp.concatenate([data] + [move(data, perm=p) for p in FIRST], axis=0)  3.88 us
  transfers between devices with their start and end apart: 19, of which 4 were waited for; matrix products, arithmetic and copies ran while one was open for 9% of the time, Pallas kernels for 0%

profile of v2, /device:TPU:1, one launch (start us, length us, event | category | flops | bytes accessed | tf_op | source)
XLA Modules:
  0.0 119.5 jit_solution(4200087878407474067)
XLA Ops:
  7.2 0.9 broadcast_select_fusion.1
  8.2 8.8 %collective-permute-start = (bf16[96,128]{1,0:T(8,128)(2,1)S(1)}, bf16[96,128]{1,0:T(8,128)(2,1)S(1)}, u32[]{:S(2)}, u32[]{:S(2)}) collective-permute-start(bf16[96,128]{1,0:T(8,128)(2,1)S(1)} %select_n.53), channel_id=1, source_target_pairs={{0,1},{1,0},{2,3},{3,2},{4,5},{5,4},{6,7},{7,6},{8,9},{9,8},{10,11... | collective-permute-start | bytes 73736 | tf_op jit(solution)/shard_map/ppermute | solution.py:123
  16.9 1.0 sub.27
  17.9 1.9 %collective-permute-start.3 = (f32[32768]{0:T(1024)S(1)}, f32[32768]{0:T(1024)S(1)}, u32[]{:S(2)}, u32[]{:S(2)}) collective-permute-start(f32[32768]{0:T(1024)S(1)} %sub.27), channel_id=1, source_target_pairs={{0,128},{128,0},{256,384},{384,256},{1,129},{129,1},{257,385},{385... | collective-permute-start | bytes 393224 | tf_op jit(solution)/shard_map/ppermute | solution.py:117
  19.9 2.5 %collective-permute-start.1 = (bf16[192,128]{1,0:T(8,128)(2,1)S(1)}, bf16[192,128]{1,0:T(8,128)(2,1)S(1)}, u32[]{:S(2)}, u32[]{:S(2)}) collective-permute-start(bf16[192,128]{1,0:T(8,128)(2,1)S(1)} %pad_maximum_fusion.2), channel_id=1, source_target_pairs={{0,2},{1,3},{2,0},{3,1},{4,6},{5,7},{6,4},{7,5},{8,10},{9,11},{10,... | collective-permute-start | bytes 147464 | tf_op jit(solution)/shard_map/ppermute | solution.py:124
  22.4 2.5 %collective-permute-done.3 = f32[32768]{0:T(1024)S(1)} collective-permute-done((f32[32768]{0:T(1024)S(1)}, f32[32768]{0:T(1024)S(1)}, u32[]{:S(2)}, u32[]{:S(2)}) %collective-permute-start.3) | collective-permute-done | bytes 131104 | tf_op jit(solution)/shard_map/ppermute | solution.py:117
  25.0 1.9 %collective-permute-start.4 = (f32[32768]{0:T(1024)S(1)}, f32[32768]{0:T(1024)S(1)}, u32[]{:S(2)}, u32[]{:S(2)}) collective-permute-start(f32[32768]{0:T(1024)S(1)} %add.106), channel_id=1, source_target_pairs={{0,256},{256,0},{128,384},{384,128},{1,257},{257,1},{129,385},{385... | collective-permute-start | bytes 393224 | tf_op jit(solution)/shard_map/ppermute | solution.py:118
  26.9 1.9 %pad_maximum_fusion = bf16[2,112,1024]{2,1,0:T(8,128)(2,1)} fusion(bf16[1,112,1024]{2,1,0:T(8,128)(2,1)} %bitcast.14, bf16[1,112,1024]{2,1,0:T(8,128)(2,1)} %bitcast.15), kind=kLoop, calls=%fused_computation | loop fusion | flops 229376 | bytes 917504 | tf_op jit(solution)/shard_map/stack | solution.py:115
  29.1 8.3 %collective-permute-start.2 = (bf16[384,128]{1,0:T(8,128)(2,1)S(1)}, bf16[384,128]{1,0:T(8,128)(2,1)S(1)}, u32[]{:S(2)}, u32[]{:S(2)}) collective-permute-start(bf16[384,128]{1,0:T(8,128)(2,1)S(1)} %pad_maximum_fusion.1), channel_id=1, source_target_pairs={{0,16},{1,17},{2,18},{3,19},{4,20},{5,21},{6,22},{7,23},{8,24},{9,... | collective-permute-start | bytes 294920 | tf_op jit(solution)/shard_map/ppermute | solution.py:125
  39.7 10.2 %collective-permute-start.7 = (bf16[24,4096]{1,0:T(8,128)(2,1)S(1)}, bf16[24,4096]{1,0:T(8,128)(2,1)S(1)}, u32[]{:S(2)}, u32[]{:S(2)}) collective-permute-start(bf16[24,4096]{1,0:T(8,128)(2,1)S(1)} %add.110), channel_id=1, source_target_pairs={{0,64},{1,25},{2,66},{3,27},{4,68},{5,29},{6,70},{7,31},{8,72},{9,... | collective-permute-start | bytes 589832 | tf_op jit(solution)/shard_map/ppermute | solution.py:127
  49.9 1.9 %collective-permute-start.6 = (bf16[24,4096]{1,0:T(8,128)(2,1)S(1)}, bf16[24,4096]{1,0:T(8,128)(2,1)S(1)}, u32[]{:S(2)}, u32[]{:S(2)}) collective-permute-start(bf16[24,4096]{1,0:T(8,128)(2,1)S(1)} %add.110), channel_id=1, source_target_pairs={{0,96},{1,29},{2,98},{3,31},{4,100},{5,1},{6,102},{7,3},{8,104},{9... | collective-permute-start | bytes 589832 | tf_op jit(solution)/shard_map/ppermute | solution.py:127
  51.8 3.4 %collective-permute-start.5 = (bf16[24,4096]{1,0:T(8,128)(2,1)S(1)}, bf16[24,4096]{1,0:T(8,128)(2,1)S(1)}, u32[]{:S(2)}, u32[]{:S(2)}) collective-permute-start(bf16[24,4096]{1,0:T(8,128)(2,1)S(1)} %add.110), channel_id=1, source_target_pairs={{0,32},{1,5},{2,34},{3,7},{4,36},{5,9},{6,38},{7,11},{8,40},{9,13}... | collective-permute-start | bytes 589832 | tf_op jit(solution)/shard_map/ppermute | solution.py:127
  55.2 0.8 constant_dynamic-update-slice_fusion.5
  55.9 3.9 %collective-permute-done.5 = bf16[24,4096]{1,0:T(8,128)(2,1)S(1)} collective-permute-done((bf16[24,4096]{1,0:T(8,128)(2,1)S(1)}, bf16[24,4096]{1,0:T(8,128)(2,1)S(1)}, u32[]{:S(2)}, u32[]{:S(2)}) %collective-permute-start.5) | collective-permute-done | bytes 196640 | tf_op jit(solution)/shard_map/ppermute | solution.py:127
  59.8 0.8 constant_dynamic-update-slice_fusion.4
  60.6 4.2 %collective-permute-start.10 = (bf16[48,4096]{1,0:T(8,128)(2,1)}, bf16[48,4096]{1,0:T(8,128)(2,1)S(1)}, u32[]{:S(2)}, u32[]{:S(2)}) collective-permute-start(bf16[48,4096]{1,0:T(8,128)(2,1)} %get-tuple-element.19), channel_id=1, source_target_pairs={{0,28},{1,97},{2,30},{3,99},{4,0},{5,101},{6,2},{7,103},{8,4},{9,1... | collective-permute-start | bytes 1179656 | tf_op jit(solution)/shard_map/ppermute | solution.py:130
  64.8 0.8 constant_dynamic-update-slice_fusion.7
  66.4 2.4 %collective-permute-start.11 = (bf16[48,4096]{1,0:T(8,128)(2,1)}, bf16[48,4096]{1,0:T(8,128)(2,1)S(1)}, u32[]{:S(2)}, u32[]{:S(2)}) collective-permute-start(bf16[48,4096]{1,0:T(8,128)(2,1)} %get-tuple-element.15), channel_id=1, source_target_pairs={{0,28},{1,97},{2,30},{3,99},{4,0},{5,101},{6,2},{7,103},{8,4},{9,1... | collective-permute-start | bytes 1179656 | tf_op jit(solution)/shard_map/ppermute | solution.py:129
  68.8 2.8 %collective-permute-start.9 = (bf16[48,4096]{1,0:T(8,128)(2,1)}, bf16[48,4096]{1,0:T(8,128)(2,1)S(1)}, u32[]{:S(2)}, u32[]{:S(2)}) collective-permute-start(bf16[48,4096]{1,0:T(8,128)(2,1)} %get-tuple-element.15), channel_id=1, source_target_pairs={{0,4},{1,33},{2,6},{3,35},{4,8},{5,37},{6,10},{7,39},{8,12},{9,41}... | collective-permute-start | bytes 1179656 | tf_op jit(solution)/shard_map/ppermute | solution.py:130
  71.7 1.9 %collective-permute-start.8 = (bf16[48,4096]{1,0:T(8,128)(2,1)}, bf16[48,4096]{1,0:T(8,128)(2,1)S(1)}, u32[]{:S(2)}, u32[]{:S(2)}) collective-permute-start(bf16[48,4096]{1,0:T(8,128)(2,1)} %get-tuple-element.19), channel_id=1, source_target_pairs={{0,4},{1,33},{2,6},{3,35},{4,8},{5,37},{6,10},{7,39},{8,12},{9,41}... | collective-permute-start | bytes 1179656 | tf_op jit(solution)/shard_map/ppermute | solution.py:129
  73.6 4.5 %collective-permute-start.14 = (bf16[96,4096]{1,0:T(8,128)(2,1)}, bf16[96,4096]{1,0:T(8,128)(2,1)}, u32[]{:S(2)}, u32[]{:S(2)}) collective-permute-start(bf16[96,4096]{1,0:T(8,128)(2,1)} %get-tuple-element.16.refs_0_), channel_id=1, source_target_pairs={{0,1},{1,0},{2,3},{3,2},{4,5},{5,4},{6,7},{7,6},{8,9},{9,8},{10,11... | collective-permute-start | bytes 2359304 | tf_op jit(solution)/shard_map/ppermute | solution.py:136
  78.2 1.2 slice.13
  80.2 3.7 %collective-permute-start.13 = (bf16[48,4096]{1,0:T(8,128)(2,1)S(1)}, bf16[48,4096]{1,0:T(8,128)(2,1)S(1)}, u32[]{:S(2)}, u32[]{:S(2)}) collective-permute-start(bf16[48,4096]{1,0:T(8,128)(2,1)S(1)} %get-tuple-element.11), channel_id=1, source_target_pairs={{0,28},{1,97},{2,30},{3,99},{4,0},{5,101},{6,2},{7,103},{8,4},{9,1... | collective-permute-start | bytes 1179656 | tf_op jit(solution)/shard_map/ppermute | solution.py:132
  84.0 0.8 broadcast_add_fusion.1
  84.8 1.9 %collective-permute-start.12 = (bf16[48,4096]{1,0:T(8,128)(2,1)S(1)}, bf16[48,4096]{1,0:T(8,128)(2,1)S(1)}, u32[]{:S(2)}, u32[]{:S(2)}) collective-permute-start(bf16[48,4096]{1,0:T(8,128)(2,1)S(1)} %get-tuple-element.13), channel_id=1, source_target_pairs={{0,4},{1,33},{2,6},{3,35},{4,8},{5,37},{6,10},{7,39},{8,12},{9,41}... | collective-permute-start | bytes 1179656 | tf_op jit(solution)/shard_map/ppermute | solution.py:132
  86.7 0.8 constant_dynamic-update-slice_fusion.8.refs_1_
  87.5 5.4 %collective-permute-start.15 = (bf16[96,4096]{1,0:T(8,128)(2,1)}, bf16[96,4096]{1,0:T(8,128)(2,1)}, u32[]{:S(2)}, u32[]{:S(2)}) collective-permute-start(bf16[96,4096]{1,0:T(8,128)(2,1)} %constant_dynamic-update-slice_fusion.8.refs_1_), channel_id=1, source_target_pairs={{0,1},{1,0},{2,3},{3,2},{4,5},{5,4},{6,7},{7,6},{8,9},{9,8},{10,11... | collective-permute-start | bytes 2359304 | tf_op jit(solution)/shard_map/ppermute | solution.py:136
  92.9 1.9 %collective-permute-start.16 = (bf16[96,4096]{1,0:T(8,128)(2,1)S(1)}, bf16[96,4096]{1,0:T(8,128)(2,1)}, u32[]{:S(2)}, u32[]{:S(2)}) collective-permute-start(bf16[96,4096]{1,0:T(8,128)(2,1)S(1)} %get-tuple-element.12.refs_2_), channel_id=1, source_target_pairs={{0,1},{1,0},{2,3},{3,2},{4,5},{5,4},{6,7},{7,6},{8,9},{9,8},{10,11... | collective-permute-start | bytes 2359304 | tf_op jit(solution)/shard_map/ppermute | solution.py:136
  95.0 6.2 %collective-permute-start.17 = (bf16[96,4096]{1,0:T(8,128)(2,1)S(1)}, bf16[96,4096]{1,0:T(8,128)(2,1)}, u32[]{:S(2)}, u32[]{:S(2)}) collective-permute-start(bf16[96,4096]{1,0:T(8,128)(2,1)S(1)} %constant_dynamic-update-slice_fusion.12.refs_3_), channel_id=1, source_target_pairs={{0,1},{1,0},{2,3},{3,2},{4,5},{5,4},{6,7},{7,6},{8,9},{9,8},{10,11... | collective-permute-start | bytes 2359304 | tf_op jit(solution)/shard_map/ppermute | solution.py:136
  101.6 1.6 %collective-permute-done.17.refs_7_ = bf16[96,4096]{1,0:T(8,128)(2,1)} collective-permute-done((bf16[96,4096]{1,0:T(8,128)(2,1)S(1)}, bf16[96,4096]{1,0:T(8,128)(2,1)}, u32[]{:S(2)}, u32[]{:S(2)}) %collective-permute-start.17) | collective-permute-done | bytes 786464 | tf_op jit(solution)/shard_map/ppermute | solution.py:136
  103.2 1.5 %copy-done.1 = bf16[8,112,1024]{2,1,0:T(8,128)(2,1)S(1)} copy-done((bf16[8,112,1024]{2,1,0:T(8,128)(2,1)S(1)}, bf16[8,112,1024]{2,1,0:T(8,128)(2,1)}, u32[]{:S(2)}) %copy-start.1) | copy-done | bytes 1835032
  104.7 7.3 %shard_map.174 = (f32[112,4096]{1,0:T(8,128)}, f32[112,1]{1,0:T(8,128)S(1)}) custom-call(s32[1]{0:T(128)} %bitcast.core_ref, s32[1,384]{1,0:T(1,128)S(1)} %broadcast_in_dim.13.idt_ref, s32[384,1]{1,0:T(8,128)S(1)} %broadcast_in_dim.16.idc_ref, bf16[4,2,112,1024]{3,2,1,0:T(8,128)(2,1)S(1)} %bitcast.13, f32[112,4096]{1,0:T(8,128)S(1)} %bitcast.11, ...), custom_call_target="tpu_custom_call" | custom-call | flops 1200000000 | bytes 12000000 | tf_op jit(solution)/shard_map/pallas_call | solution.py:140
  (60 shorter events, 3.9 us)
Async XLA Ops:
  7.2 30.3 %copy-start.2 = (f32[32768]{0:T(1024)S(1)}, f32[32768]{0:T(1024)}, u32[]{:S(2)}) copy-start(f32[32768]{0:T(1024)} %param.21) | copy-start | bytes 393220
  7.2 30.3 %copy-start.3 = (f32[32768]{0:T(1024)S(1)}, f32[32768]{0:T(1024)}, u32[]{:S(2)}) copy-start(f32[32768]{0:T(1024)} %param.23) | copy-start | bytes 393220
  7.2 71.0 %all-gather.3.cloned.1.call-start = ((), (), s32[]{:S(2)}) async-start(), calls=%async_computation | async-start | bytes 2293760 | tf_op jit(solution)/shard_map/all_gather | solution.py:115
  8.2 11.8 %collective-permute-start = (bf16[96,128]{1,0:T(8,128)(2,1)S(1)}, bf16[96,128]{1,0:T(8,128)(2,1)S(1)}, u32[]{:S(2)}, u32[]{:S(2)}) collective-permute-start(bf16[96,128]{1,0:T(8,128)(2,1)S(1)} %select_n.53), channel_id=1, source_target_pairs={{0,1},{1,0},{2,3},{3,2},{4,5},{5,4},{6,7},{7,6},{8,9},{9,8},{10,11... | collective-permute-start | bytes 73736 | tf_op jit(solution)/shard_map/ppermute | solution.py:123
  17.9 7.0 %collective-permute-start.3 = (f32[32768]{0:T(1024)S(1)}, f32[32768]{0:T(1024)S(1)}, u32[]{:S(2)}, u32[]{:S(2)}) collective-permute-start(f32[32768]{0:T(1024)S(1)} %sub.27), channel_id=1, source_target_pairs={{0,128},{128,0},{256,384},{384,256},{1,129},{129,1},{257,385},{385... | collective-permute-start | bytes 393224 | tf_op jit(solution)/shard_map/ppermute | solution.py:117
  19.9 9.2 %collective-permute-start.1 = (bf16[192,128]{1,0:T(8,128)(2,1)S(1)}, bf16[192,128]{1,0:T(8,128)(2,1)S(1)}, u32[]{:S(2)}, u32[]{:S(2)}) collective-permute-start(bf16[192,128]{1,0:T(8,128)(2,1)S(1)} %pad_maximum_fusion.2), channel_id=1, source_target_pairs={{0,2},{1,3},{2,0},{3,1},{4,6},{5,7},{6,4},{7,5},{8,10},{9,11},{10,... | collective-permute-start | bytes 147464 | tf_op jit(solution)/shard_map/ppermute | solution.py:124
  25.0 12.5 %collective-permute-start.4 = (f32[32768]{0:T(1024)S(1)}, f32[32768]{0:T(1024)S(1)}, u32[]{:S(2)}, u32[]{:S(2)}) collective-permute-start(f32[32768]{0:T(1024)S(1)} %add.106), channel_id=1, source_target_pairs={{0,256},{256,0},{128,384},{384,128},{1,257},{257,1},{129,385},{385... | collective-permute-start | bytes 393224 | tf_op jit(solution)/shard_map/ppermute | solution.py:118
  29.1 10.4 %collective-permute-start.2 = (bf16[384,128]{1,0:T(8,128)(2,1)S(1)}, bf16[384,128]{1,0:T(8,128)(2,1)S(1)}, u32[]{:S(2)}, u32[]{:S(2)}) collective-permute-start(bf16[384,128]{1,0:T(8,128)(2,1)S(1)} %pad_maximum_fusion.1), channel_id=1, source_target_pairs={{0,16},{1,17},{2,18},{3,19},{4,20},{5,21},{6,22},{7,23},{8,24},{9,... | collective-permute-start | bytes 294920 | tf_op jit(solution)/shard_map/ppermute | solution.py:125
  39.7 26.0 %collective-permute-start.7 = (bf16[24,4096]{1,0:T(8,128)(2,1)S(1)}, bf16[24,4096]{1,0:T(8,128)(2,1)S(1)}, u32[]{:S(2)}, u32[]{:S(2)}) collective-permute-start(bf16[24,4096]{1,0:T(8,128)(2,1)S(1)} %add.110), channel_id=1, source_target_pairs={{0,64},{1,25},{2,66},{3,27},{4,68},{5,29},{6,70},{7,31},{8,72},{9,... | collective-permute-start | bytes 589832 | tf_op jit(solution)/shard_map/ppermute | solution.py:127
  49.9 15.0 %collective-permute-start.6 = (bf16[24,4096]{1,0:T(8,128)(2,1)S(1)}, bf16[24,4096]{1,0:T(8,128)(2,1)S(1)}, u32[]{:S(2)}, u32[]{:S(2)}) collective-permute-start(bf16[24,4096]{1,0:T(8,128)(2,1)S(1)} %add.110), channel_id=1, source_target_pairs={{0,96},{1,29},{2,98},{3,31},{4,100},{5,1},{6,102},{7,3},{8,104},{9... | collective-permute-start | bytes 589832 | tf_op jit(solution)/shard_map/ppermute | solution.py:127
  51.8 8.0 %collective-permute-start.5 = (bf16[24,4096]{1,0:T(8,128)(2,1)S(1)}, bf16[24,4096]{1,0:T(8,128)(2,1)S(1)}, u32[]{:S(2)}, u32[]{:S(2)}) collective-permute-start(bf16[24,4096]{1,0:T(8,128)(2,1)S(1)} %add.110), channel_id=1, source_target_pairs={{0,32},{1,5},{2,34},{3,7},{4,36},{5,9},{6,38},{7,11},{8,40},{9,13}... | collective-permute-start | bytes 589832 | tf_op jit(solution)/shard_map/ppermute | solution.py:127
  60.6 17.5 %collective-permute-start.10 = (bf16[48,4096]{1,0:T(8,128)(2,1)}, bf16[48,4096]{1,0:T(8,128)(2,1)S(1)}, u32[]{:S(2)}, u32[]{:S(2)}) collective-permute-start(bf16[48,4096]{1,0:T(8,128)(2,1)} %get-tuple-element.19), channel_id=1, source_target_pairs={{0,28},{1,97},{2,30},{3,99},{4,0},{5,101},{6,2},{7,103},{8,4},{9,1... | collective-permute-start | bytes 1179656 | tf_op jit(solution)/shard_map/ppermute | solution.py:130
  66.4 13.7 %collective-permute-start.11 = (bf16[48,4096]{1,0:T(8,128)(2,1)}, bf16[48,4096]{1,0:T(8,128)(2,1)S(1)}, u32[]{:S(2)}, u32[]{:S(2)}) collective-permute-start(bf16[48,4096]{1,0:T(8,128)(2,1)} %get-tuple-element.15), channel_id=1, source_target_pairs={{0,28},{1,97},{2,30},{3,99},{4,0},{5,101},{6,2},{7,103},{8,4},{9,1... | collective-permute-start | bytes 1179656 | tf_op jit(solution)/shard_map/ppermute | solution.py:129
  68.8 17.9 %collective-permute-start.9 = (bf16[48,4096]{1,0:T(8,128)(2,1)}, bf16[48,4096]{1,0:T(8,128)(2,1)S(1)}, u32[]{:S(2)}, u32[]{:S(2)}) collective-permute-start(bf16[48,4096]{1,0:T(8,128)(2,1)} %get-tuple-element.15), channel_id=1, source_target_pairs={{0,4},{1,33},{2,6},{3,35},{4,8},{5,37},{6,10},{7,39},{8,12},{9,41}... | collective-permute-start | bytes 1179656 | tf_op jit(solution)/shard_map/ppermute | solution.py:130
  71.7 12.3 %collective-permute-start.8 = (bf16[48,4096]{1,0:T(8,128)(2,1)}, bf16[48,4096]{1,0:T(8,128)(2,1)S(1)}, u32[]{:S(2)}, u32[]{:S(2)}) collective-permute-start(bf16[48,4096]{1,0:T(8,128)(2,1)} %get-tuple-element.19), channel_id=1, source_target_pairs={{0,4},{1,33},{2,6},{3,35},{4,8},{5,37},{6,10},{7,39},{8,12},{9,41}... | collective-permute-start | bytes 1179656 | tf_op jit(solution)/shard_map/ppermute | solution.py:129
  73.6 28.0 %collective-permute-start.14 = (bf16[96,4096]{1,0:T(8,128)(2,1)}, bf16[96,4096]{1,0:T(8,128)(2,1)}, u32[]{:S(2)}, u32[]{:S(2)}) collective-permute-start(bf16[96,4096]{1,0:T(8,128)(2,1)} %get-tuple-element.16.refs_0_), channel_id=1, source_target_pairs={{0,1},{1,0},{2,3},{3,2},{4,5},{5,4},{6,7},{7,6},{8,9},{9,8},{10,11... | collective-permute-start | bytes 2359304 | tf_op jit(solution)/shard_map/ppermute | solution.py:136
  80.1 21.1 %copy-start.4 = (s32[384]{0:T(512)S(1)}, s32[384]{0:T(512)}, u32[]{:S(2)}) copy-start(s32[384]{0:T(512)} %constant.108) | copy-start | bytes 4612
  80.1 21.1 %copy-start.5 = (s32[384]{0:T(512)S(1)}, s32[384]{0:T(512)}, u32[]{:S(2)}) copy-start(s32[384]{0:T(512)} %constant.99.clone) | copy-start | bytes 4612
  80.2 21.1 %copy-start.6 = (s32[384]{0:T(512)S(1)}, s32[384]{0:T(512)}, u32[]{:S(2)}) copy-start(s32[384]{0:T(512)} %constant.98.clone) | copy-start | bytes 4612
  80.2 21.1 %copy-start.7 = (s32[384]{0:T(512)S(1)}, s32[384]{0:T(512)}, u32[]{:S(2)}) copy-start(s32[384]{0:T(512)} %constant.97.clone) | copy-start | bytes 4612
  80.2 21.1 %copy-start.8 = (s32[384]{0:T(512)S(1)}, s32[384]{0:T(512)}, u32[]{:S(2)}) copy-start(s32[384]{0:T(512)} %constant.96.clone) | copy-start | bytes 4612
  80.2 21.1 %copy-start.9 = (s32[384]{0:T(512)S(1)}, s32[384]{0:T(512)}, u32[]{:S(2)}) copy-start(s32[384]{0:T(512)} %constant.95.clone) | copy-start | bytes 4612
  80.2 21.1 %copy-start.10 = (s32[384]{0:T(512)S(1)}, s32[384]{0:T(512)}, u32[]{:S(2)}) copy-start(s32[384]{0:T(512)} %constant.94.clone) | copy-start | bytes 4612
  80.2 21.1 %copy-start.11 = (f32[1,112]{1,0:T(1,128)S(1)}, f32[1,112]{1,0:T(1,128)}, u32[]{:S(2)}) copy-start(f32[1,112]{1,0:T(1,128)} %param.20) | copy-start | bytes 1348
  80.2 23.0 %copy-start = (f32[1,112,4096]{2,1,0:T(8,128)S(1)}, f32[1,112,4096]{2,1,0:T(8,128)}, u32[]{:S(2)}) copy-start(f32[1,112,4096]{2,1,0:T(8,128)} %param.19) | copy-start | bytes 5505028
  80.2 14.7 %collective-permute-start.13 = (bf16[48,4096]{1,0:T(8,128)(2,1)S(1)}, bf16[48,4096]{1,0:T(8,128)(2,1)S(1)}, u32[]{:S(2)}, u32[]{:S(2)}) collective-permute-start(bf16[48,4096]{1,0:T(8,128)(2,1)S(1)} %get-tuple-element.11), channel_id=1, source_target_pairs={{0,28},{1,97},{2,30},{3,99},{4,0},{5,101},{6,2},{7,103},{8,4},{9,1... | collective-permute-start | bytes 1179656 | tf_op jit(solution)/shard_map/ppermute | solution.py:132
  84.8 10.1 %collective-permute-start.12 = (bf16[48,4096]{1,0:T(8,128)(2,1)S(1)}, bf16[48,4096]{1,0:T(8,128)(2,1)S(1)}, u32[]{:S(2)}, u32[]{:S(2)}) collective-permute-start(bf16[48,4096]{1,0:T(8,128)(2,1)S(1)} %get-tuple-element.13), channel_id=1, source_target_pairs={{0,4},{1,33},{2,6},{3,35},{4,8},{5,37},{6,10},{7,39},{8,12},{9,41}... | collective-permute-start | bytes 1179656 | tf_op jit(solution)/shard_map/ppermute | solution.py:132
  87.5 14.1 %collective-permute-start.15 = (bf16[96,4096]{1,0:T(8,128)(2,1)}, bf16[96,4096]{1,0:T(8,128)(2,1)}, u32[]{:S(2)}, u32[]{:S(2)}) collective-permute-start(bf16[96,4096]{1,0:T(8,128)(2,1)} %constant_dynamic-update-slice_fusion.8.refs_1_), channel_id=1, source_target_pairs={{0,1},{1,0},{2,3},{3,2},{4,5},{5,4},{6,7},{7,6},{8,9},{9,8},{10,11... | collective-permute-start | bytes 2359304 | tf_op jit(solution)/shard_map/ppermute | solution.py:136
  92.9 8.7 %collective-permute-start.16 = (bf16[96,4096]{1,0:T(8,128)(2,1)S(1)}, bf16[96,4096]{1,0:T(8,128)(2,1)}, u32[]{:S(2)}, u32[]{:S(2)}) collective-permute-start(bf16[96,4096]{1,0:T(8,128)(2,1)S(1)} %get-tuple-element.12.refs_2_), channel_id=1, source_target_pairs={{0,1},{1,0},{2,3},{3,2},{4,5},{5,4},{6,7},{7,6},{8,9},{9,8},{10,11... | collective-permute-start | bytes 2359304 | tf_op jit(solution)/shard_map/ppermute | solution.py:136
  95.0 8.2 %collective-permute-start.17 = (bf16[96,4096]{1,0:T(8,128)(2,1)S(1)}, bf16[96,4096]{1,0:T(8,128)(2,1)}, u32[]{:S(2)}, u32[]{:S(2)}) collective-permute-start(bf16[96,4096]{1,0:T(8,128)(2,1)S(1)} %constant_dynamic-update-slice_fusion.12.refs_3_), channel_id=1, source_target_pairs={{0,1},{1,0},{2,3},{3,2},{4,5},{5,4},{6,7},{7,6},{8,9},{9,8},{10,11... | collective-permute-start | bytes 2359304 | tf_op jit(solution)/shard_map/ppermute | solution.py:136
  103.2 1.5 %copy-start.1 = (bf16[8,112,1024]{2,1,0:T(8,128)(2,1)S(1)}, bf16[8,112,1024]{2,1,0:T(8,128)(2,1)}, u32[]{:S(2)}) copy-start(bf16[8,112,1024]{2,1,0:T(8,128)(2,1)} %all-gather.3.cloned.1.call-done) | copy-start | bytes 5505028
Sparse Core Ops, SparseCore 0:
  28.9 48.4 all-gather.2

commit v3 on v2

v3 whole, which is shorter than its diff:
```python
import functools

import jax
import jax.numpy as jnp
import numpy as np
from jax import lax
from jax.experimental import pallas as pl
from jax.experimental.pallas import tpu as pltpu
from jax.sharding import PartitionSpec as P

NX, NZ = 4, 8
BF = jnp.bfloat16
F32 = jnp.float32
ROWS_BY_ROWS = (((1,), (1,)), ((), ()))


def flat(x, z, h, c):
    return (((x % NX) * NZ + z % NZ) * 2 + h) * 2 + c


def pairs(target):
    return [
        (flat(x, z, h, c), flat(*target(x, z, h, c)))
        for x in range(NX)
        for z in range(NZ)
        for h in range(2)
        for c in range(2)
    ]


SWAP = pairs(lambda x, z, h, c: (x, z, h, 1 - c))
HALF = pairs(lambda x, z, h, c: (x, z, 1 - h, c))
FAR = pairs(lambda x, z, h, c: (x, z ^ 4, h, c))
FIRST = tuple(
    pairs(lambda x, z, h, c, s=s: (x, z + s, h, c) if c else (x + s, z, h, c)) for s in (1, -1, -2)
)
UP = pairs(lambda x, z, h, c: (x + 1, z, h, c) if c else (x, z + 1, h, c))
DOWN = pairs(lambda x, z, h, c: (x - 1, z, h, c) if c else (x, z - 1, h, c))


def row_tables():
    row = np.arange(96)
    early = np.array([0, -1, 1, 2])[row // 24]
    ring = np.concatenate([np.zeros(96), -np.ones(96), np.ones(96), np.where(row < 48, -2, 2)])
    inner = [np.tile(v, 4) for v in (early, row // 12 % 2 * 4, row // 6 % 2, row // 3 % 2, row % 3)]
    return [jnp.asarray(v.astype(np.int32)) for v in (ring, *inner)]


def row_ids(me):
    ring, early, four, half, core, r = row_tables()
    x, z, h = me // 32, me // 4 % 8, me // 2 % 2
    h = h ^ half
    tokens = (((((x + early) & 3) * 8 + (((z + ring) & 7) ^ four)) * 2 + h) * 2 + core) * 3 + r
    cots = (((((x + ring) & 3) * 8 + (((z + early) & 7) ^ four)) * 2 + h) * 2 + (1 - core)) * 3 + r
    return tokens[None, :], cots[:, None]


def fetch(refs, buf, sems, base):
    copies, row = [], 0
    for k, ref in enumerate(refs):
        rows = ref.shape[0]
        copies.append(pltpu.make_async_copy(ref, buf.at[pl.ds(row, rows), :], sems.at[base + k]))
        copies[-1].start()
        row += rows
    return copies


def hidden_rows(tok, w_ref):
    both = None
    for j in range(4):
        part = lax.dot_general(
            tok[:, j * 1024 : (j + 1) * 1024],
            w_ref[j].reshape(224, 1024),
            ROWS_BY_ROWS,
            preferred_element_type=F32,
        )
        both = part if both is None else both + part
    gate, up = both[:, :112], both[:, 112:]
    return (gate / (1.0 + jnp.exp(-gate)) * up).astype(BF)


def early_kernel(core_ref, w_ref, *refs):
    own, oth, (hid_ref, tok, sems) = refs[:3], refs[3:6], refs[6:]
    for which, blocks in enumerate((own, oth)):

        @pl.when(core_ref[0] == which)
        def _(blocks=blocks):
            for copy in fetch(blocks, tok, sems, 0):
                copy.wait()

    hid_ref[...] = hidden_rows(tok, w_ref)


def late_kernel(core_ref, idt_ref, idc_ref, hid_ref, w_ref, dm_ref, sm_ref, *refs):
    own, oth, (nd_ref, ns_ref, hid, tok, cot, sems) = refs[:5], refs[5:10], refs[10:]
    eye = lax.broadcasted_iota(jnp.int32, (112, 112), 0) == lax.broadcasted_iota(jnp.int32, (112, 112), 1)
    for which, (toks, cots) in enumerate(((own, oth), (oth, own))):

        @pl.when(core_ref[0] == which)
        def _(toks=toks, cots=cots):
            first, second = fetch(toks[3:], tok, sems, 0), fetch(cots, cot, sems, 2)
            for copy in first:
                copy.wait()
            hid[...] = hidden_rows(tok, w_ref)
            for copy in second:
                copy.wait()

    rows = jnp.concatenate([hid_ref[...], hid[...]], axis=0)
    pick = (idc_ref[...] == idt_ref[...]).astype(F32).astype(BF)
    turned = lax.dot_general(rows, pick, (((0,), (1,)), ((), ())), preferred_element_type=F32).astype(BF)
    total = jnp.zeros((112, 1), F32)
    step = 512
    for d in range(0, 4096, step):
        grad = jnp.dot(turned, cot[:, d : d + step], preferred_element_type=F32)
        nd_ref[:, d : d + step] = grad
        total = total + jnp.sum(grad * grad, axis=1, keepdims=True)
    before = jnp.sum(jnp.where(eye, sm_ref[...], 0.0), axis=1, keepdims=True)
    second = 0.95 * before + 0.05 * (total * (1.0 / 4096.0))
    ns_ref[...] = jnp.sum(jnp.where(eye, second, 0.0), axis=0, keepdims=True)
    scale = 0.3 / (jnp.sqrt(second) + 1e-08)
    for d in range(0, 4096, step):
        nd_ref[:, d : d + step] = dm_ref[:, d : d + step] - nd_ref[:, d : d + step] * scale


def local(
    tokens,
    cotangent,
    w_gate,
    w_up,
    down_master,
    second_moment,
    outer_params,
    inner_params,
    outer_momentum,
):
    me = lax.axis_index("fsdp")
    core = me % 2
    move = functools.partial(lax.ppermute, axis_name="fsdp")

    weights = lax.all_gather(jnp.stack([w_gate, w_up]), "island", axis=0, tiled=False)
    tok, cot = tokens.reshape(96, 128), cotangent.reshape(96, 128)
    mine = jnp.where(core == 0, tok, cot)
    give = jnp.where(core == 0, cot, tok)
    came = move(give, perm=SWAP)
    data = jnp.concatenate([mine, came], axis=0)
    difference = outer_params - inner_params[0]
    pair = difference + lax.ppermute(difference, "island", ((0, 1), (1, 0), (2, 3), (3, 2)))
    total = pair + lax.ppermute(pair, "island", ((0, 2), (2, 0), (1, 3), (3, 1)))
    data = jnp.concatenate([data, move(data, perm=HALF)], axis=0)
    data = jnp.concatenate([data, move(data, perm=FAR)], axis=0) + (total[0] * 0).astype(BF)
    data = data.reshape(24, 4096)
    data = jnp.concatenate([data] + [move(data, perm=p) for p in FIRST], axis=0)
    tie = weights[0, 0, 0, 0] * 0
    below, above = move(data, perm=UP), move(data, perm=DOWN)
    far_lo, far_hi = move(below[:48], perm=UP), move(above[48:] + tie, perm=DOWN)
    own = (data, below, above, far_lo, far_hi)
    oth = tuple(move(v, perm=SWAP) for v in own)

    idt, idc = row_ids(me)
    vmem = pl.BlockSpec(memory_space=pltpu.VMEM)
    smem = pl.BlockSpec(memory_space=pltpu.SMEM)
    anywhere = pl.BlockSpec(memory_space=pl.ANY)
    params = pltpu.CompilerParams(vmem_limit_bytes=20 * 2**20)
    hid = pl.pallas_call(
        early_kernel,
        out_shape=jax.ShapeDtypeStruct((288, 112), BF),
        in_specs=[smem, vmem] + [anywhere] * 6,
        out_specs=vmem,
        scratch_shapes=[pltpu.VMEM((288, 4096), BF), pltpu.SemaphoreType.DMA((3,))],
        compiler_params=params,
        cost_estimate=pl.CostEstimate(flops=530_000_000, bytes_accessed=6_500_000, transcendentals=32256),
    )(core[None], weights, *own[:3], *oth[:3])
    new_down, new_second = pl.pallas_call(
        late_kernel,
        out_shape=(jax.ShapeDtypeStruct((112, 4096), F32), jax.ShapeDtypeStruct((1, 112), F32)),
        in_specs=[smem] + [vmem] * 6 + [anywhere] * 10,
        out_specs=(vmem, vmem),
        scratch_shapes=[
            pltpu.VMEM((96, 112), BF),
            pltpu.VMEM((96, 4096), BF),
            pltpu.VMEM((384, 4096), BF),
            pltpu.SemaphoreType.DMA((7,)),
        ],
        compiler_params=params,
        cost_estimate=pl.CostEstimate(flops=530_000_000, bytes_accessed=9_000_000, transcendentals=10752),
    )(core[None], idt, idc, hid, weights, down_master[0], second_moment, *own, *oth)

    pseudo = total / lax.axis_size("island")
    new_momentum = 0.9 * outer_momentum + pseudo
    new_outer = outer_params - 0.7 * (pseudo + 0.9 * new_momentum)
    return (new_down[None], new_second, new_outer, new_momentum)


def solution(mesh):
    placed = (
        P("island", "fsdp", None),
        P("island", "fsdp", None),
        P("fsdp", "island"),
        P("fsdp", "island"),
        P("island", "fsdp", None),
        P("island", "fsdp"),
        P("fsdp"),
        P("island", "fsdp"),
        P("fsdp"),
    )
    return jax.shard_map(
        local,
        mesh=mesh,
        in_specs=placed,
        out_specs=(P("island", "fsdp", None), P("island", "fsdp"), P("fsdp"), P("fsdp")),
        check_vma=False,
    )
```

time: 120 us -> 115 us (0.958)
  starting transfers between devices: 74 us -> 68.1 us
  waiting for transfers between devices: 8.42 us -> 13.3 us
  local copies, waits for them, and re-layouts: 7.74 us -> 4.36 us
    ppermute x7 -> x5, waiting for transfers between devices: 0.02 us -> 5.56 us  [the longest x2 4.2 us: local(): below, above = (move(data, perm=UP), move(data, perm=DOWN))]
    ppermute x7 -> x5, starting transfers between devices: 25.8 us -> 20.4 us  [the longest x1 8.79 us: local(): came = move(give, perm=SWAP)]
    unnamed x28 -> x21, local copies, waits for them, and re-layouts: 3.2 us -> 1.58 us
    ppermute x4 -> x5, waiting for transfers between devices: 1.61 us -> 0.01 us  [local(): oth = tuple((move(v, perm=SWAP) for v in own))]
    concatenate x2 -> x1, local copies, waits for them, and re-layouts: 1.54 us -> 0.02 us  [local(): data = jnp.concatenate([data] + [move(data, perm=p) for p in FIRST], axis=0)]
    ppermute x4 -> x5, starting transfers between devices: 18.1 us -> 17.6 us  [local(): oth = tuple((move(v, perm=SWAP) for v in own))]
    pallas_call x1 -> x2, Pallas kernels: 7.33 us -> 6.89 us  [the longest x1 4.45 us: local(): pl.pallas_call(late_kernel, out_shape=(jax.ShapeDtypeStruct((112, 4096),...]
  transfers between devices with their start and end apart: 19 -> 18, of which waited for: 4 -> 6; matrix products, arithmetic and copies ran while one was open for 9% -> 6% of each run, Pallas kernels for 0% -> 2%
where the time goes in v3:
time: 115 us; the launch traced here: 114 us
  starting transfers between devices  68.1 us (59%)
  between operations  15.9 us (14%)
  waiting for transfers between devices  13.3 us (12%)
  Pallas kernels  6.89 us (6%)
  other arithmetic  5.27 us (5%)
  local copies, waits for them, and re-layouts  4.36 us (4%)
    ppermute x5, starting transfers between devices, local(): oth = tuple((move(v, perm=SWAP) for v in own))  17.6 us
    ppermute x3, starting transfers between devices, local(): data = jnp.concatenate([data] + [move(data, perm=p) for p in FIRST], axis=0)  15.5 us
    ppermute x1, starting transfers between devices, local(): came = move(give, perm=SWAP)  8.79 us
    ppermute x1, starting transfers between devices, local(): move(data, perm=FAR)  8.31 us
    ppermute x2, starting transfers between devices, local(): below, above = (move(data, perm=UP), move(data, perm=DOWN))  6.49 us
    ppermute x3, waiting for transfers between devices, local(): data = jnp.concatenate([data] + [move(data, perm=p) for p in FIRST], axis=0)  4.64 us
    pallas_call x1, Pallas kernels, local(): pl.pallas_call(late_kernel, out_shape=(jax.ShapeDtypeStruct((112, 4096),...  4.45 us
    ppermute x2, waiting for transfers between devices, local(): below, above = (move(data, perm=UP), move(data, perm=DOWN))  4.2 us
  transfers between devices with their start and end apart: 18, of which 6 were waited for; matrix products, arithmetic and copies ran while one was open for 6% of the time, Pallas kernels for 2%

profile of v3, /device:TPU:1, one launch (start us, length us, event | category | flops | bytes accessed | tf_op | source)
XLA Modules:
  0.0 113.8 jit_solution(11672142653994181515)
XLA Ops:
  7.2 0.9 broadcast_select_fusion.1
  8.2 8.8 %collective-permute-start = (bf16[96,128]{1,0:T(8,128)(2,1)S(1)}, bf16[96,128]{1,0:T(8,128)(2,1)S(1)}, u32[]{:S(2)}, u32[]{:S(2)}) collective-permute-start(bf16[96,128]{1,0:T(8,128)(2,1)S(1)} %select_n.53), channel_id=1, source_target_pairs={{0,1},{1,0},{2,3},{3,2},{4,5},{5,4},{6,7},{7,6},{8,9},{9,8},{10,11... | collective-permute-start | bytes 73736 | tf_op jit(solution)/shard_map/ppermute | solution.py:144
  16.9 1.0 sub.27
  17.9 1.9 %collective-permute-start.3 = (f32[32768]{0:T(1024)S(1)}, f32[32768]{0:T(1024)S(1)}, u32[]{:S(2)}, u32[]{:S(2)}) collective-permute-start(f32[32768]{0:T(1024)S(1)} %sub.27), channel_id=1, source_target_pairs={{0,128},{128,0},{256,384},{384,256},{1,129},{129,1},{257,385},{385... | collective-permute-start | bytes 393224 | tf_op jit(solution)/shard_map/ppermute | solution.py:147
  19.9 2.5 %collective-permute-start.1 = (bf16[192,128]{1,0:T(8,128)(2,1)S(1)}, bf16[192,128]{1,0:T(8,128)(2,1)S(1)}, u32[]{:S(2)}, u32[]{:S(2)}) collective-permute-start(bf16[192,128]{1,0:T(8,128)(2,1)S(1)} %pad_maximum_fusion.2), channel_id=1, source_target_pairs={{0,2},{1,3},{2,0},{3,1},{4,6},{5,7},{6,4},{7,5},{8,10},{9,11},{10,... | collective-permute-start | bytes 147464 | tf_op jit(solution)/shard_map/ppermute | solution.py:149
  22.4 2.5 %collective-permute-done.3 = f32[32768]{0:T(1024)S(1)} collective-permute-done((f32[32768]{0:T(1024)S(1)}, f32[32768]{0:T(1024)S(1)}, u32[]{:S(2)}, u32[]{:S(2)}) %collective-permute-start.3) | collective-permute-done | bytes 131104 | tf_op jit(solution)/shard_map/ppermute | solution.py:147
  25.0 1.9 %collective-permute-start.4 = (f32[32768]{0:T(1024)S(1)}, f32[32768]{0:T(1024)S(1)}, u32[]{:S(2)}, u32[]{:S(2)}) collective-permute-start(f32[32768]{0:T(1024)S(1)} %add.102), channel_id=1, source_target_pairs={{0,256},{256,0},{128,384},{384,128},{1,257},{257,1},{129,385},{385... | collective-permute-start | bytes 393224 | tf_op jit(solution)/shard_map/ppermute | solution.py:148
  26.9 1.9 %pad_maximum_fusion = bf16[2,112,1024]{2,1,0:T(8,128)(2,1)} fusion(bf16[1,112,1024]{2,1,0:T(8,128)(2,1)} %bitcast.13, bf16[1,112,1024]{2,1,0:T(8,128)(2,1)} %bitcast.14), kind=kLoop, calls=%fused_computation | loop fusion | flops 229376 | bytes 917504 | tf_op jit(solution)/shard_map/stack | solution.py:140
  29.1 8.3 %collective-permute-start.2 = (bf16[384,128]{1,0:T(8,128)(2,1)S(1)}, bf16[384,128]{1,0:T(8,128)(2,1)S(1)}, u32[]{:S(2)}, u32[]{:S(2)}) collective-permute-start(bf16[384,128]{1,0:T(8,128)(2,1)S(1)} %pad_maximum_fusion.1), channel_id=1, source_target_pairs={{0,16},{1,17},{2,18},{3,19},{4,20},{5,21},{6,22},{7,23},{8,24},{9,... | collective-permute-start | bytes 294920 | tf_op jit(solution)/shard_map/ppermute | solution.py:150
  37.5 0.7 multiply_subtract_fusion
  38.2 0.5 slice.16
  39.7 10.2 %collective-permute-start.7 = (bf16[24,4096]{1,0:T(8,128)(2,1)S(1)}, bf16[24,4096]{1,0:T(8,128)(2,1)S(1)}, u32[]{:S(2)}, u32[]{:S(2)}) collective-permute-start(bf16[24,4096]{1,0:T(8,128)(2,1)S(1)} %add.106), channel_id=1, source_target_pairs={{0,64},{1,25},{2,66},{3,27},{4,68},{5,29},{6,70},{7,31},{8,72},{9,... | collective-permute-start | bytes 589832 | tf_op jit(solution)/shard_map/ppermute | solution.py:152
  49.9 1.9 %collective-permute-start.6 = (bf16[24,4096]{1,0:T(8,128)(2,1)S(1)}, bf16[24,4096]{1,0:T(8,128)(2,1)S(1)}, u32[]{:S(2)}, u32[]{:S(2)}) collective-permute-start(bf16[24,4096]{1,0:T(8,128)(2,1)S(1)} %add.106), channel_id=1, source_target_pairs={{0,96},{1,29},{2,98},{3,31},{4,100},{5,1},{6,102},{7,3},{8,104},{9... | collective-permute-start | bytes 589832 | tf_op jit(solution)/shard_map/ppermute | solution.py:152
  51.8 3.4 %collective-permute-start.5 = (bf16[24,4096]{1,0:T(8,128)(2,1)S(1)}, bf16[24,4096]{1,0:T(8,128)(2,1)S(1)}, u32[]{:S(2)}, u32[]{:S(2)}) collective-permute-start(bf16[24,4096]{1,0:T(8,128)(2,1)S(1)} %add.106), channel_id=1, source_target_pairs={{0,32},{1,5},{2,34},{3,7},{4,36},{5,9},{6,38},{7,11},{8,40},{9,13}... | collective-permute-start | bytes 589832 | tf_op jit(solution)/shard_map/ppermute | solution.py:152
  55.2 4.6 %collective-permute-done.5 = bf16[24,4096]{1,0:T(8,128)(2,1)S(1)} collective-permute-done((bf16[24,4096]{1,0:T(8,128)(2,1)S(1)}, bf16[24,4096]{1,0:T(8,128)(2,1)S(1)}, u32[]{:S(2)}, u32[]{:S(2)}) %collective-permute-start.5) | collective-permute-done | bytes 196640 | tf_op jit(solution)/shard_map/ppermute | solution.py:152
  59.9 3.0 %collective-permute-start.8 = (bf16[96,4096]{1,0:T(8,128)(2,1)S(1)}, bf16[96,4096]{1,0:T(8,128)(2,1)S(1)}, u32[]{:S(2)}, u32[]{:S(2)}) collective-permute-start(bf16[96,4096]{1,0:T(8,128)(2,1)S(1)} %constant_dynamic-update-slice_fusion.refs_0_), channel_id=1, source_target_pairs={{0,4},{1,33},{2,6},{3,35},{4,8},{5,37},{6,10},{7,39},{8,12},{9,41}... | collective-permute-start | bytes 2359304 | tf_op jit(solution)/shard_map/ppermute | solution.py:154
  62.9 3.5 %collective-permute-start.9 = (bf16[96,4096]{1,0:T(8,128)(2,1)S(1)}, bf16[96,4096]{1,0:T(8,128)(2,1)S(1)}, u32[]{:S(2)}, u32[]{:S(2)}) collective-permute-start(bf16[96,4096]{1,0:T(8,128)(2,1)S(1)} %constant_dynamic-update-slice_fusion.refs_0_), channel_id=1, source_target_pairs={{0,28},{1,97},{2,30},{3,99},{4,0},{5,101},{6,2},{7,103},{8,4},{9,1... | collective-permute-start | bytes 2359304 | tf_op jit(solution)/shard_map/ppermute | solution.py:154
  66.5 3.6 %collective-permute-start.10 = (bf16[96,4096]{1,0:T(8,128)(2,1)S(1)}, bf16[96,4096]{1,0:T(8,128)(2,1)S(1)}, u32[]{:S(2)}, u32[]{:S(2)}) collective-permute-start(bf16[96,4096]{1,0:T(8,128)(2,1)S(1)} %constant_dynamic-update-slice_fusion.refs_0_), channel_id=1, source_target_pairs={{0,1},{1,0},{2,3},{3,2},{4,5},{5,4},{6,7},{7,6},{8,9},{9,8},{10,11... | collective-permute-start | bytes 2359304 | tf_op jit(solution)/shard_map/ppermute | solution.py:157
  70.1 4.2 %collective-permute-done.8.refs_1_ = bf16[96,4096]{1,0:T(8,128)(2,1)S(1)} collective-permute-done((bf16[96,4096]{1,0:T(8,128)(2,1)S(1)}, bf16[96,4096]{1,0:T(8,128)(2,1)S(1)}, u32[]{:S(2)}, u32[]{:S(2)}) %collective-permute-start.8) | collective-permute-done | bytes 786464 | tf_op jit(solution)/shard_map/ppermute | solution.py:154
  74.3 0.8 slice.17
  75.1 1.9 %collective-permute-start.13 = (bf16[48,4096]{1,0:T(8,128)(2,1)}, bf16[48,4096]{1,0:T(8,128)(2,1)S(1)}, u32[]{:S(2)}, u32[]{:S(2)}) collective-permute-start(bf16[48,4096]{1,0:T(8,128)(2,1)} %slice.17), channel_id=1, source_target_pairs={{0,4},{1,33},{2,6},{3,35},{4,8},{5,37},{6,10},{7,39},{8,12},{9,41}... | collective-permute-start | bytes 1179656 | tf_op jit(solution)/shard_map/ppermute | solution.py:155
  77.0 3.8 %collective-permute-start.11 = (bf16[96,4096]{1,0:T(8,128)(2,1)S(1)}, bf16[96,4096]{1,0:T(8,128)(2,1)}, u32[]{:S(2)}, u32[]{:S(2)}) collective-permute-start(bf16[96,4096]{1,0:T(8,128)(2,1)S(1)} %collective-permute-done.8.refs_1_), channel_id=1, source_target_pairs={{0,1},{1,0},{2,3},{3,2},{4,5},{5,4},{6,7},{7,6},{8,9},{9,8},{10,11... | collective-permute-start | bytes 2359304 | tf_op jit(solution)/shard_map/ppermute | solution.py:157
  80.8 1.9 %collective-permute-start.12 = (bf16[96,4096]{1,0:T(8,128)(2,1)S(1)}, bf16[96,4096]{1,0:T(8,128)(2,1)}, u32[]{:S(2)}, u32[]{:S(2)}) collective-permute-start(bf16[96,4096]{1,0:T(8,128)(2,1)S(1)} %collective-permute-done.9.refs_2_), channel_id=1, source_target_pairs={{0,1},{1,0},{2,3},{3,2},{4,5},{5,4},{6,7},{7,6},{8,9},{9,8},{10,11... | collective-permute-start | bytes 2359304 | tf_op jit(solution)/shard_map/ppermute | solution.py:157
  82.8 1.2 %slice.19 = bf16[1,1,1,1]{3,2,1,0:T(2,128)(2,1)} slice(bf16[4,2,112,1024]{3,2,1,0:T(8,128)(2,1)} %bitcast.9), slice={[0:1], [0:1], [0:1], [0:1]} | slice | bytes 4 | tf_op jit(solution)/shard_map/slice | solution.py:153
  84.7 3.2 %collective-permute-start.14 = (bf16[48,4096]{1,0:T(8,128)(2,1)S(1)}, bf16[48,4096]{1,0:T(8,128)(2,1)}, u32[]{:S(2)}, u32[]{:S(2)}) collective-permute-start(bf16[48,4096]{1,0:T(8,128)(2,1)S(1)} %slice_add_fusion), channel_id=1, source_target_pairs={{0,28},{1,97},{2,30},{3,99},{4,0},{5,101},{6,2},{7,103},{8,4},{9,1... | collective-permute-start | bytes 1179656 | tf_op jit(solution)/shard_map/ppermute | solution.py:155
  87.8 4.4 %collective-permute-start.15 = (bf16[48,4096]{1,0:T(8,128)(2,1)S(1)}, bf16[48,4096]{1,0:T(8,128)(2,1)}, u32[]{:S(2)}, u32[]{:S(2)}) collective-permute-start(bf16[48,4096]{1,0:T(8,128)(2,1)S(1)} %collective-permute-done.13.refs_3_), channel_id=1, source_target_pairs={{0,1},{1,0},{2,3},{3,2},{4,5},{5,4},{6,7},{7,6},{8,9},{9,8},{10,11... | collective-permute-start | bytes 1179656 | tf_op jit(solution)/shard_map/ppermute | solution.py:157
  92.2 1.4 %collective-permute-done.14.refs_4_ = bf16[48,4096]{1,0:T(8,128)(2,1)} collective-permute-done((bf16[48,4096]{1,0:T(8,128)(2,1)S(1)}, bf16[48,4096]{1,0:T(8,128)(2,1)}, u32[]{:S(2)}, u32[]{:S(2)}) %collective-permute-start.14) | collective-permute-done | bytes 393248 | tf_op jit(solution)/shard_map/ppermute | solution.py:155
  93.6 3.9 %collective-permute-start.16 = (bf16[48,4096]{1,0:T(8,128)(2,1)}, bf16[48,4096]{1,0:T(8,128)(2,1)}, u32[]{:S(2)}, u32[]{:S(2)}) collective-permute-start(bf16[48,4096]{1,0:T(8,128)(2,1)} %collective-permute-done.14.refs_4_), channel_id=1, source_target_pairs={{0,1},{1,0},{2,3},{3,2},{4,5},{5,4},{6,7},{7,6},{8,9},{9,8},{10,11... | collective-permute-start | bytes 1179656 | tf_op jit(solution)/shard_map/ppermute | solution.py:157
  97.6 0.7 fusion.7
  98.5 1.5 %copy-done = bf16[8,112,1024]{2,1,0:T(8,128)(2,1)S(1)} copy-done((bf16[8,112,1024]{2,1,0:T(8,128)(2,1)S(1)}, bf16[8,112,1024]{2,1,0:T(8,128)(2,1)}, u32[]{:S(2)}) %copy-start) | copy-done | bytes 1835032
  100.0 2.4 %shard_map.174.hid_ref = bf16[288,112]{1,0:T(8,128)(2,1)S(1)} custom-call(s32[1]{0:T(128)} %bitcast.core_ref, bf16[4,2,112,1024]{3,2,1,0:T(8,128)(2,1)S(1)} %bitcast.10, bf16[96,4096]{1,0:T(8,128)(2,1)S(1)} %constant_dynamic-update-slice_fusion.refs_0_, bf16[96,4096]{1,0:T(8,128)(2,1)S(1)} %collective-permute-done.8.refs_1_, ...), custom_call_target="tpu_custom_call" | custom-call | flops 530000000 | bytes 6500000 | tf_op jit(solution)/shard_map/pallas_call | solution.py:164
  102.4 4.4 %shard_map.175 = (f32[112,4096]{1,0:T(8,128)}, f32[1,112]{1,0:T(1,128)}) custom-call(s32[1]{0:T(128)} %bitcast.core_ref, s32[1,384]{1,0:T(1,128)S(1)} %broadcast_in_dim.14.idt_ref, s32[384,1]{1,0:T(8,128)S(1)} %broadcast_in_dim.17.idc_ref, bf16[288,112]{1,0:T(8,128)(2,1)S(1)} %shard_map.174.hid_ref, bf16[4,2,112,1024]{3,2,1,0:T(8,128)(2,1)S(1)} %bitcast.11, ...), custom_call_target="tpu_custom_call" | custom-call | flops 530000000 | bytes 9000000 | tf_op jit(solution)/shard_map/pallas_call | solution.py:173
  (47 shorter events, 1.1 us)
Async XLA Ops:
  7.2 30.3 %copy-start.3 = (f32[32768]{0:T(1024)S(1)}, f32[32768]{0:T(1024)}, u32[]{:S(2)}) copy-start(f32[32768]{0:T(1024)} %param.21) | copy-start | bytes 393220
  7.2 30.3 %copy-start.4 = (f32[32768]{0:T(1024)S(1)}, f32[32768]{0:T(1024)}, u32[]{:S(2)}) copy-start(f32[32768]{0:T(1024)} %param.23) | copy-start | bytes 393220
  7.2 75.6 %all-gather.3.cloned.1.call-start = ((), (), s32[]{:S(2)}) async-start(), calls=%async_computation | async-start | bytes 2293760 | tf_op jit(solution)/shard_map/all_gather | solution.py:140
  8.2 11.8 %collective-permute-start = (bf16[96,128]{1,0:T(8,128)(2,1)S(1)}, bf16[96,128]{1,0:T(8,128)(2,1)S(1)}, u32[]{:S(2)}, u32[]{:S(2)}) collective-permute-start(bf16[96,128]{1,0:T(8,128)(2,1)S(1)} %select_n.53), channel_id=1, source_target_pairs={{0,1},{1,0},{2,3},{3,2},{4,5},{5,4},{6,7},{7,6},{8,9},{9,8},{10,11... | collective-permute-start | bytes 73736 | tf_op jit(solution)/shard_map/ppermute | solution.py:144
  17.9 7.0 %collective-permute-start.3 = (f32[32768]{0:T(1024)S(1)}, f32[32768]{0:T(1024)S(1)}, u32[]{:S(2)}, u32[]{:S(2)}) collective-permute-start(f32[32768]{0:T(1024)S(1)} %sub.27), channel_id=1, source_target_pairs={{0,128},{128,0},{256,384},{384,256},{1,129},{129,1},{257,385},{385... | collective-permute-start | bytes 393224 | tf_op jit(solution)/shard_map/ppermute | solution.py:147
  19.9 9.2 %collective-permute-start.1 = (bf16[192,128]{1,0:T(8,128)(2,1)S(1)}, bf16[192,128]{1,0:T(8,128)(2,1)S(1)}, u32[]{:S(2)}, u32[]{:S(2)}) collective-permute-start(bf16[192,128]{1,0:T(8,128)(2,1)S(1)} %pad_maximum_fusion.2), channel_id=1, source_target_pairs={{0,2},{1,3},{2,0},{3,1},{4,6},{5,7},{6,4},{7,5},{8,10},{9,11},{10,... | collective-permute-start | bytes 147464 | tf_op jit(solution)/shard_map/ppermute | solution.py:149
  25.0 12.5 %collective-permute-start.4 = (f32[32768]{0:T(1024)S(1)}, f32[32768]{0:T(1024)S(1)}, u32[]{:S(2)}, u32[]{:S(2)}) collective-permute-start(f32[32768]{0:T(1024)S(1)} %add.102), channel_id=1, source_target_pairs={{0,256},{256,0},{128,384},{384,128},{1,257},{257,1},{129,385},{385... | collective-permute-start | bytes 393224 | tf_op jit(solution)/shard_map/ppermute | solution.py:148
  29.1 10.4 %collective-permute-start.2 = (bf16[384,128]{1,0:T(8,128)(2,1)S(1)}, bf16[384,128]{1,0:T(8,128)(2,1)S(1)}, u32[]{:S(2)}, u32[]{:S(2)}) collective-permute-start(bf16[384,128]{1,0:T(8,128)(2,1)S(1)} %pad_maximum_fusion.1), channel_id=1, source_target_pairs={{0,16},{1,17},{2,18},{3,19},{4,20},{5,21},{6,22},{7,23},{8,24},{9,... | collective-permute-start | bytes 294920 | tf_op jit(solution)/shard_map/ppermute | solution.py:150
  39.6 58.0 %copy-start.5 = (s32[384]{0:T(512)S(1)}, s32[384]{0:T(512)}, u32[]{:S(2)}) copy-start(s32[384]{0:T(512)} %constant.108) | copy-start | bytes 4612
  39.6 58.0 %copy-start.6 = (s32[384]{0:T(512)S(1)}, s32[384]{0:T(512)}, u32[]{:S(2)}) copy-start(s32[384]{0:T(512)} %constant.99.clone) | copy-start | bytes 4612
  39.6 58.0 %copy-start.7 = (s32[384]{0:T(512)S(1)}, s32[384]{0:T(512)}, u32[]{:S(2)}) copy-start(s32[384]{0:T(512)} %constant.98.clone) | copy-start | bytes 4612
  39.6 58.0 %copy-start.8 = (s32[384]{0:T(512)S(1)}, s32[384]{0:T(512)}, u32[]{:S(2)}) copy-start(s32[384]{0:T(512)} %constant.97.clone) | copy-start | bytes 4612
  39.7 20.2 %collective-permute-start.7 = (bf16[24,4096]{1,0:T(8,128)(2,1)S(1)}, bf16[24,4096]{1,0:T(8,128)(2,1)S(1)}, u32[]{:S(2)}, u32[]{:S(2)}) collective-permute-start(bf16[24,4096]{1,0:T(8,128)(2,1)S(1)} %add.106), channel_id=1, source_target_pairs={{0,64},{1,25},{2,66},{3,27},{4,68},{5,29},{6,70},{7,31},{8,72},{9,... | collective-permute-start | bytes 589832 | tf_op jit(solution)/shard_map/ppermute | solution.py:152
  49.9 10.0 %collective-permute-start.6 = (bf16[24,4096]{1,0:T(8,128)(2,1)S(1)}, bf16[24,4096]{1,0:T(8,128)(2,1)S(1)}, u32[]{:S(2)}, u32[]{:S(2)}) collective-permute-start(bf16[24,4096]{1,0:T(8,128)(2,1)S(1)} %add.106), channel_id=1, source_target_pairs={{0,96},{1,29},{2,98},{3,31},{4,100},{5,1},{6,102},{7,3},{8,104},{9... | collective-permute-start | bytes 589832 | tf_op jit(solution)/shard_map/ppermute | solution.py:152
  51.8 8.0 %collective-permute-start.5 = (bf16[24,4096]{1,0:T(8,128)(2,1)S(1)}, bf16[24,4096]{1,0:T(8,128)(2,1)S(1)}, u32[]{:S(2)}, u32[]{:S(2)}) collective-permute-start(bf16[24,4096]{1,0:T(8,128)(2,1)S(1)} %add.106), channel_id=1, source_target_pairs={{0,32},{1,5},{2,34},{3,7},{4,36},{5,9},{6,38},{7,11},{8,40},{9,13}... | collective-permute-start | bytes 589832 | tf_op jit(solution)/shard_map/ppermute | solution.py:152
  59.9 14.3 %collective-permute-start.8 = (bf16[96,4096]{1,0:T(8,128)(2,1)S(1)}, bf16[96,4096]{1,0:T(8,128)(2,1)S(1)}, u32[]{:S(2)}, u32[]{:S(2)}) collective-permute-start(bf16[96,4096]{1,0:T(8,128)(2,1)S(1)} %constant_dynamic-update-slice_fusion.refs_0_), channel_id=1, source_target_pairs={{0,4},{1,33},{2,6},{3,35},{4,8},{5,37},{6,10},{7,39},{8,12},{9,41}... | collective-permute-start | bytes 2359304 | tf_op jit(solution)/shard_map/ppermute | solution.py:154
  62.9 17.9 %collective-permute-start.9 = (bf16[96,4096]{1,0:T(8,128)(2,1)S(1)}, bf16[96,4096]{1,0:T(8,128)(2,1)S(1)}, u32[]{:S(2)}, u32[]{:S(2)}) collective-permute-start(bf16[96,4096]{1,0:T(8,128)(2,1)S(1)} %constant_dynamic-update-slice_fusion.refs_0_), channel_id=1, source_target_pairs={{0,28},{1,97},{2,30},{3,99},{4,0},{5,101},{6,2},{7,103},{8,4},{9,1... | collective-permute-start | bytes 2359304 | tf_op jit(solution)/shard_map/ppermute | solution.py:154
  66.5 32.0 %collective-permute-start.10 = (bf16[96,4096]{1,0:T(8,128)(2,1)S(1)}, bf16[96,4096]{1,0:T(8,128)(2,1)S(1)}, u32[]{:S(2)}, u32[]{:S(2)}) collective-permute-start(bf16[96,4096]{1,0:T(8,128)(2,1)S(1)} %constant_dynamic-update-slice_fusion.refs_0_), channel_id=1, source_target_pairs={{0,1},{1,0},{2,3},{3,2},{4,5},{5,4},{6,7},{7,6},{8,9},{9,8},{10,11... | collective-permute-start | bytes 2359304 | tf_op jit(solution)/shard_map/ppermute | solution.py:157
  75.1 12.8 %collective-permute-start.13 = (bf16[48,4096]{1,0:T(8,128)(2,1)}, bf16[48,4096]{1,0:T(8,128)(2,1)S(1)}, u32[]{:S(2)}, u32[]{:S(2)}) collective-permute-start(bf16[48,4096]{1,0:T(8,128)(2,1)} %slice.17), channel_id=1, source_target_pairs={{0,4},{1,33},{2,6},{3,35},{4,8},{5,37},{6,10},{7,39},{8,12},{9,41}... | collective-permute-start | bytes 1179656 | tf_op jit(solution)/shard_map/ppermute | solution.py:155
  77.0 21.5 %collective-permute-start.11 = (bf16[96,4096]{1,0:T(8,128)(2,1)S(1)}, bf16[96,4096]{1,0:T(8,128)(2,1)}, u32[]{:S(2)}, u32[]{:S(2)}) collective-permute-start(bf16[96,4096]{1,0:T(8,128)(2,1)S(1)} %collective-permute-done.8.refs_1_), channel_id=1, source_target_pairs={{0,1},{1,0},{2,3},{3,2},{4,5},{5,4},{6,7},{7,6},{8,9},{9,8},{10,11... | collective-permute-start | bytes 2359304 | tf_op jit(solution)/shard_map/ppermute | solution.py:157
  80.8 17.6 %collective-permute-start.12 = (bf16[96,4096]{1,0:T(8,128)(2,1)S(1)}, bf16[96,4096]{1,0:T(8,128)(2,1)}, u32[]{:S(2)}, u32[]{:S(2)}) collective-permute-start(bf16[96,4096]{1,0:T(8,128)(2,1)S(1)} %collective-permute-done.9.refs_2_), channel_id=1, source_target_pairs={{0,1},{1,0},{2,3},{3,2},{4,5},{5,4},{6,7},{7,6},{8,9},{9,8},{10,11... | collective-permute-start | bytes 2359304 | tf_op jit(solution)/shard_map/ppermute | solution.py:157
  84.7 8.9 %collective-permute-start.14 = (bf16[48,4096]{1,0:T(8,128)(2,1)S(1)}, bf16[48,4096]{1,0:T(8,128)(2,1)}, u32[]{:S(2)}, u32[]{:S(2)}) collective-permute-start(bf16[48,4096]{1,0:T(8,128)(2,1)S(1)} %slice_add_fusion), channel_id=1, source_target_pairs={{0,28},{1,97},{2,30},{3,99},{4,0},{5,101},{6,2},{7,103},{8,4},{9,1... | collective-permute-start | bytes 1179656 | tf_op jit(solution)/shard_map/ppermute | solution.py:155
  87.8 14.6 %collective-permute-start.15 = (bf16[48,4096]{1,0:T(8,128)(2,1)S(1)}, bf16[48,4096]{1,0:T(8,128)(2,1)}, u32[]{:S(2)}, u32[]{:S(2)}) collective-permute-start(bf16[48,4096]{1,0:T(8,128)(2,1)S(1)} %collective-permute-done.13.refs_3_), channel_id=1, source_target_pairs={{0,1},{1,0},{2,3},{3,2},{4,5},{5,4},{6,7},{7,6},{8,9},{9,8},{10,11... | collective-permute-start | bytes 1179656 | tf_op jit(solution)/shard_map/ppermute | solution.py:157
  93.6 8.8 %collective-permute-start.16 = (bf16[48,4096]{1,0:T(8,128)(2,1)}, bf16[48,4096]{1,0:T(8,128)(2,1)}, u32[]{:S(2)}, u32[]{:S(2)}) collective-permute-start(bf16[48,4096]{1,0:T(8,128)(2,1)} %collective-permute-done.14.refs_4_), channel_id=1, source_target_pairs={{0,1},{1,0},{2,3},{3,2},{4,5},{5,4},{6,7},{7,6},{8,9},{9,8},{10,11... | collective-permute-start | bytes 1179656 | tf_op jit(solution)/shard_map/ppermute | solution.py:157
  98.5 1.5 %copy-start = (bf16[8,112,1024]{2,1,0:T(8,128)(2,1)S(1)}, bf16[8,112,1024]{2,1,0:T(8,128)(2,1)}, u32[]{:S(2)}) copy-start(bf16[8,112,1024]{2,1,0:T(8,128)(2,1)} %all-gather.3.cloned.1.call-done) | copy-start | bytes 5505028
  100.0 2.5 %copy-start.1 = (f32[1,112,4096]{2,1,0:T(8,128)S(1)}, f32[1,112,4096]{2,1,0:T(8,128)}, u32[]{:S(2)}) copy-start(f32[1,112,4096]{2,1,0:T(8,128)} %param.19) | copy-start | bytes 5505028
  100.0 2.5 %copy-start.2 = (f32[1,112]{1,0:T(1,128)S(1)}, f32[1,112]{1,0:T(1,128)}, u32[]{:S(2)}) copy-start(f32[1,112]{1,0:T(1,128)} %sm_ref.1) | copy-start | bytes 1348
Sparse Core Ops, SparseCore 0:
  28.9 48.4 all-gather.2

commit v4 on v3

--- a/solution.py
+++ b/solution.py
@@ -77,6 +77,13 @@
         both = part if both is None else both + part
     gate, up = both[:, :112], both[:, 112:]
     return (gate / (1.0 + jnp.exp(-gate)) * up).astype(BF)
+
+
+def keep_kernel(w_hbm, w_ref, zero_ref, sem):
+    copy = pltpu.make_async_copy(w_hbm, w_ref, sem)
+    copy.start()
+    copy.wait()
+    zero_ref[...] = w_ref[0, 0, :16, :128] * 0
 
 
 def early_kernel(core_ref, w_ref, *refs):
@@ -150,16 +157,25 @@
     data = jnp.concatenate([data, move(data, perm=FAR)], axis=0) + (total[0] * 0).astype(BF)
     data = data.reshape(24, 4096)
     data = jnp.concatenate([data] + [move(data, perm=p) for p in FIRST], axis=0)
-    tie = weights[0, 0, 0, 0] * 0
+    vmem = pl.BlockSpec(memory_space=pltpu.VMEM)
+    anywhere = pl.BlockSpec(memory_space=pl.ANY)
+    weights, zero = pl.pallas_call(
+        keep_kernel,
+        out_shape=(jax.ShapeDtypeStruct((4, 2, 112, 1024), BF), jax.ShapeDtypeStruct((16, 128), BF)),
+        in_specs=[anywhere],
+        out_specs=(vmem, vmem),
+        scratch_shapes=[pltpu.SemaphoreType.DMA],
+        compiler_params=pltpu.CompilerParams(vmem_limit_bytes=8 * 2**20),
+        cost_estimate=pl.CostEstimate(flops=2048, bytes_accessed=3_700_000, transcendentals=0),
+    )(weights)
+    tie = zero[0, 0]
     below, above = move(data, perm=UP), move(data, perm=DOWN)
     far_lo, far_hi = move(below[:48], perm=UP), move(above[48:] + tie, perm=DOWN)
     own = (data, below, above, far_lo, far_hi)
     oth = tuple(move(v, perm=SWAP) for v in own)
 
     idt, idc = row_ids(me)
-    vmem = pl.BlockSpec(memory_space=pltpu.VMEM)
     smem = pl.BlockSpec(memory_space=pltpu.SMEM)
-    anywhere = pl.BlockSpec(memory_space=pl.ANY)
     params = pltpu.CompilerParams(vmem_limit_bytes=20 * 2**20)
     hid = pl.pallas_call(
         early_kernel,

time: 115 us -> 116 us (level)
  local copies, waits for them, and re-layouts: 4.36 us -> 6.41 us
    unnamed x21 -> x27, local copies, waits for them, and re-layouts: 1.58 us -> 3.64 us
  transfers between devices with their start and end apart: 18 -> 18, of which waited for: 6 -> 6; matrix products, arithmetic and copies ran while one was open for 6% -> 8% of each run, Pallas kernels for 2% -> 2%
where the time goes in v4:
time: 116 us; the launch traced here: 115 us
  starting transfers between devices  68.2 us (59%)
  between operations  15.2 us (13%)
  waiting for transfers between devices  12.8 us (11%)
  Pallas kernels  7.23 us (6%)
  local copies, waits for them, and re-layouts  6.41 us (6%)
  other arithmetic  5.2 us (4%)
    ppermute x5, starting transfers between devices, local(): oth = tuple((move(v, perm=SWAP) for v in own))  17.6 us
    ppermute x3, starting transfers between devices, local(): data = jnp.concatenate([data] + [move(data, perm=p) for p in FIRST], axis=0)  15.5 us
    ppermute x1, starting transfers between devices, local(): came = move(give, perm=SWAP)  8.79 us
    ppermute x1, starting transfers between devices, local(): move(data, perm=FAR)  8.31 us
    ppermute x2, starting transfers between devices, local(): below, above = (move(data, perm=UP), move(data, perm=DOWN))  6.62 us
    pallas_call x1, Pallas kernels, local(): pl.pallas_call(late_kernel, out_shape=(jax.ShapeDtypeStruct((112, 4096),...  4.45 us
    ppermute x2, waiting for transfers between devices, local(): below, above = (move(data, perm=UP), move(data, perm=DOWN))  4.41 us
    ppermute x3, waiting for transfers between devices, local(): data = jnp.concatenate([data] + [move(data, perm=p) for p in FIRST], axis=0)  3.97 us
  transfers between devices with their start and end apart: 18, of which 6 were waited for; matrix products, arithmetic and copies ran while one was open for 8% of the time, Pallas kernels for 2%

profile of v4, /device:TPU:1, one launch (start us, length us, event | category | flops | bytes accessed | tf_op | source)
XLA Modules:
  0.0 115.1 jit_solution(7328360763249006964)
XLA Ops:
  7.2 0.9 broadcast_select_fusion.1
  8.2 8.8 %collective-permute-start = (bf16[96,128]{1,0:T(8,128)(2,1)S(1)}, bf16[96,128]{1,0:T(8,128)(2,1)S(1)}, u32[]{:S(2)}, u32[]{:S(2)}) collective-permute-start(bf16[96,128]{1,0:T(8,128)(2,1)S(1)} %select_n.53), channel_id=1, source_target_pairs={{0,1},{1,0},{2,3},{3,2},{4,5},{5,4},{6,7},{7,6},{8,9},{9,8},{10,11... | collective-permute-start | bytes 73736 | tf_op jit(solution)/shard_map/ppermute | solution.py:151
  16.9 1.0 sub.27
  17.9 1.9 %collective-permute-start.3 = (f32[32768]{0:T(1024)S(1)}, f32[32768]{0:T(1024)S(1)}, u32[]{:S(2)}, u32[]{:S(2)}) collective-permute-start(f32[32768]{0:T(1024)S(1)} %sub.27), channel_id=1, source_target_pairs={{0,128},{128,0},{256,384},{384,256},{1,129},{129,1},{257,385},{385... | collective-permute-start | bytes 393224 | tf_op jit(solution)/shard_map/ppermute | solution.py:154
  19.9 2.5 %collective-permute-start.1 = (bf16[192,128]{1,0:T(8,128)(2,1)S(1)}, bf16[192,128]{1,0:T(8,128)(2,1)S(1)}, u32[]{:S(2)}, u32[]{:S(2)}) collective-permute-start(bf16[192,128]{1,0:T(8,128)(2,1)S(1)} %pad_maximum_fusion.2), channel_id=1, source_target_pairs={{0,2},{1,3},{2,0},{3,1},{4,6},{5,7},{6,4},{7,5},{8,10},{9,11},{10,... | collective-permute-start | bytes 147464 | tf_op jit(solution)/shard_map/ppermute | solution.py:156
  22.4 2.5 %collective-permute-done.3 = f32[32768]{0:T(1024)S(1)} collective-permute-done((f32[32768]{0:T(1024)S(1)}, f32[32768]{0:T(1024)S(1)}, u32[]{:S(2)}, u32[]{:S(2)}) %collective-permute-start.3) | collective-permute-done | bytes 131104 | tf_op jit(solution)/shard_map/ppermute | solution.py:154
  25.0 1.9 %collective-permute-start.4 = (f32[32768]{0:T(1024)S(1)}, f32[32768]{0:T(1024)S(1)}, u32[]{:S(2)}, u32[]{:S(2)}) collective-permute-start(f32[32768]{0:T(1024)S(1)} %add.102), channel_id=1, source_target_pairs={{0,256},{256,0},{128,384},{384,128},{1,257},{257,1},{129,385},{385... | collective-permute-start | bytes 393224 | tf_op jit(solution)/shard_map/ppermute | solution.py:155
  26.9 1.9 %pad_maximum_fusion = bf16[2,112,1024]{2,1,0:T(8,128)(2,1)} fusion(bf16[1,112,1024]{2,1,0:T(8,128)(2,1)} %bitcast.11, bf16[1,112,1024]{2,1,0:T(8,128)(2,1)} %bitcast.12), kind=kLoop, calls=%fused_computation | loop fusion | flops 229376 | bytes 917504 | tf_op jit(solution)/shard_map/stack | solution.py:147
  29.1 8.3 %collective-permute-start.2 = (bf16[384,128]{1,0:T(8,128)(2,1)S(1)}, bf16[384,128]{1,0:T(8,128)(2,1)S(1)}, u32[]{:S(2)}, u32[]{:S(2)}) collective-permute-start(bf16[384,128]{1,0:T(8,128)(2,1)S(1)} %pad_maximum_fusion.1), channel_id=1, source_target_pairs={{0,16},{1,17},{2,18},{3,19},{4,20},{5,21},{6,22},{7,23},{8,24},{9,... | collective-permute-start | bytes 294920 | tf_op jit(solution)/shard_map/ppermute | solution.py:157
  37.5 0.7 multiply_subtract_fusion
  39.7 10.2 %collective-permute-start.7 = (bf16[24,4096]{1,0:T(8,128)(2,1)S(1)}, bf16[24,4096]{1,0:T(8,128)(2,1)S(1)}, u32[]{:S(2)}, u32[]{:S(2)}) collective-permute-start(bf16[24,4096]{1,0:T(8,128)(2,1)S(1)} %add.106), channel_id=1, source_target_pairs={{0,64},{1,25},{2,66},{3,27},{4,68},{5,29},{6,70},{7,31},{8,72},{9,... | collective-permute-start | bytes 589832 | tf_op jit(solution)/shard_map/ppermute | solution.py:159
  49.9 1.9 %collective-permute-start.6 = (bf16[24,4096]{1,0:T(8,128)(2,1)S(1)}, bf16[24,4096]{1,0:T(8,128)(2,1)S(1)}, u32[]{:S(2)}, u32[]{:S(2)}) collective-permute-start(bf16[24,4096]{1,0:T(8,128)(2,1)S(1)} %add.106), channel_id=1, source_target_pairs={{0,96},{1,29},{2,98},{3,31},{4,100},{5,1},{6,102},{7,3},{8,104},{9... | collective-permute-start | bytes 589832 | tf_op jit(solution)/shard_map/ppermute | solution.py:159
  51.8 3.4 %collective-permute-start.5 = (bf16[24,4096]{1,0:T(8,128)(2,1)S(1)}, bf16[24,4096]{1,0:T(8,128)(2,1)S(1)}, u32[]{:S(2)}, u32[]{:S(2)}) collective-permute-start(bf16[24,4096]{1,0:T(8,128)(2,1)S(1)} %add.106), channel_id=1, source_target_pairs={{0,32},{1,5},{2,34},{3,7},{4,36},{5,9},{6,38},{7,11},{8,40},{9,13}... | collective-permute-start | bytes 589832 | tf_op jit(solution)/shard_map/ppermute | solution.py:159
  55.2 0.7 constant_dynamic-update-slice_fusion.3
  55.8 4.0 %collective-permute-done.5 = bf16[24,4096]{1,0:T(8,128)(2,1)S(1)} collective-permute-done((bf16[24,4096]{1,0:T(8,128)(2,1)S(1)}, bf16[24,4096]{1,0:T(8,128)(2,1)S(1)}, u32[]{:S(2)}, u32[]{:S(2)}) %collective-permute-start.5) | collective-permute-done | bytes 196640 | tf_op jit(solution)/shard_map/ppermute | solution.py:159
  59.8 0.7 constant_dynamic-update-slice_fusion.2
  60.5 0.7 constant_dynamic-update-slice_fusion.1
  61.9 3.1 %collective-permute-start.8 = (bf16[96,4096]{1,0:T(8,128)(2,1)}, bf16[96,4096]{1,0:T(8,128)(2,1)S(1)}, u32[]{:S(2)}, u32[]{:S(2)}) collective-permute-start(bf16[96,4096]{1,0:T(8,128)(2,1)} %constant_dynamic-update-slice_fusion.refs_0_), channel_id=1, source_target_pairs={{0,4},{1,33},{2,6},{3,35},{4,8},{5,37},{6,10},{7,39},{8,12},{9,41}... | collective-permute-start | bytes 2359304 | tf_op jit(solution)/shard_map/ppermute | solution.py:172
  65.0 3.5 %collective-permute-start.9 = (bf16[96,4096]{1,0:T(8,128)(2,1)}, bf16[96,4096]{1,0:T(8,128)(2,1)S(1)}, u32[]{:S(2)}, u32[]{:S(2)}) collective-permute-start(bf16[96,4096]{1,0:T(8,128)(2,1)} %constant_dynamic-update-slice_fusion.refs_0_), channel_id=1, source_target_pairs={{0,28},{1,97},{2,30},{3,99},{4,0},{5,101},{6,2},{7,103},{8,4},{9,1... | collective-permute-start | bytes 2359304 | tf_op jit(solution)/shard_map/ppermute | solution.py:172
  68.6 3.6 %collective-permute-start.10 = (bf16[96,4096]{1,0:T(8,128)(2,1)}, bf16[96,4096]{1,0:T(8,128)(2,1)}, u32[]{:S(2)}, u32[]{:S(2)}) collective-permute-start(bf16[96,4096]{1,0:T(8,128)(2,1)} %constant_dynamic-update-slice_fusion.refs_0_), channel_id=1, source_target_pairs={{0,1},{1,0},{2,3},{3,2},{4,5},{5,4},{6,7},{7,6},{8,9},{9,8},{10,11... | collective-permute-start | bytes 2359304 | tf_op jit(solution)/shard_map/ppermute | solution.py:175
  72.2 4.4 %collective-permute-done.8.refs_1_ = bf16[96,4096]{1,0:T(8,128)(2,1)S(1)} collective-permute-done((bf16[96,4096]{1,0:T(8,128)(2,1)}, bf16[96,4096]{1,0:T(8,128)(2,1)S(1)}, u32[]{:S(2)}, u32[]{:S(2)}) %collective-permute-start.8) | collective-permute-done | bytes 786464 | tf_op jit(solution)/shard_map/ppermute | solution.py:172
  76.6 0.8 slice.17
  77.4 1.9 %collective-permute-start.13 = (bf16[48,4096]{1,0:T(8,128)(2,1)}, bf16[48,4096]{1,0:T(8,128)(2,1)}, u32[]{:S(2)}, u32[]{:S(2)}) collective-permute-start(bf16[48,4096]{1,0:T(8,128)(2,1)} %slice.17), channel_id=1, source_target_pairs={{0,4},{1,33},{2,6},{3,35},{4,8},{5,37},{6,10},{7,39},{8,12},{9,41}... | collective-permute-start | bytes 1179656 | tf_op jit(solution)/shard_map/ppermute | solution.py:173
  79.3 3.8 %collective-permute-start.11 = (bf16[96,4096]{1,0:T(8,128)(2,1)S(1)}, bf16[96,4096]{1,0:T(8,128)(2,1)}, u32[]{:S(2)}, u32[]{:S(2)}) collective-permute-start(bf16[96,4096]{1,0:T(8,128)(2,1)S(1)} %collective-permute-done.8.refs_1_), channel_id=1, source_target_pairs={{0,1},{1,0},{2,3},{3,2},{4,5},{5,4},{6,7},{7,6},{8,9},{9,8},{10,11... | collective-permute-start | bytes 2359304 | tf_op jit(solution)/shard_map/ppermute | solution.py:175
  83.2 1.9 %collective-permute-start.12 = (bf16[96,4096]{1,0:T(8,128)(2,1)S(1)}, bf16[96,4096]{1,0:T(8,128)(2,1)}, u32[]{:S(2)}, u32[]{:S(2)}) collective-permute-start(bf16[96,4096]{1,0:T(8,128)(2,1)S(1)} %collective-permute-done.9.refs_2_), channel_id=1, source_target_pairs={{0,1},{1,0},{2,3},{3,2},{4,5},{5,4},{6,7},{7,6},{8,9},{9,8},{10,11... | collective-permute-start | bytes 2359304 | tf_op jit(solution)/shard_map/ppermute | solution.py:175
  85.1 1.5 %copy-done.1 = bf16[8,112,1024]{2,1,0:T(8,128)(2,1)S(1)} copy-done((bf16[8,112,1024]{2,1,0:T(8,128)(2,1)S(1)}, bf16[8,112,1024]{2,1,0:T(8,128)(2,1)}, u32[]{:S(2)}) %copy-start.1) | copy-done | bytes 1835032
  88.0 3.2 %collective-permute-start.14 = (bf16[48,4096]{1,0:T(8,128)(2,1)S(1)}, bf16[48,4096]{1,0:T(8,128)(2,1)}, u32[]{:S(2)}, u32[]{:S(2)}) collective-permute-start(bf16[48,4096]{1,0:T(8,128)(2,1)S(1)} %slice_add_fusion), channel_id=1, source_target_pairs={{0,28},{1,97},{2,30},{3,99},{4,0},{5,101},{6,2},{7,103},{8,4},{9,1... | collective-permute-start | bytes 1179656 | tf_op jit(solution)/shard_map/ppermute | solution.py:173
  91.1 4.4 %collective-permute-start.15 = (bf16[48,4096]{1,0:T(8,128)(2,1)}, bf16[48,4096]{1,0:T(8,128)(2,1)}, u32[]{:S(2)}, u32[]{:S(2)}) collective-permute-start(bf16[48,4096]{1,0:T(8,128)(2,1)} %collective-permute-done.13.refs_3_), channel_id=1, source_target_pairs={{0,1},{1,0},{2,3},{3,2},{4,5},{5,4},{6,7},{7,6},{8,9},{9,8},{10,11... | collective-permute-start | bytes 1179656 | tf_op jit(solution)/shard_map/ppermute | solution.py:175
  95.5 1.4 %collective-permute-done.14.refs_4_ = bf16[48,4096]{1,0:T(8,128)(2,1)} collective-permute-done((bf16[48,4096]{1,0:T(8,128)(2,1)S(1)}, bf16[48,4096]{1,0:T(8,128)(2,1)}, u32[]{:S(2)}, u32[]{:S(2)}) %collective-permute-start.14) | collective-permute-done | bytes 393248 | tf_op jit(solution)/shard_map/ppermute | solution.py:173
  96.9 3.9 %collective-permute-start.16 = (bf16[48,4096]{1,0:T(8,128)(2,1)}, bf16[48,4096]{1,0:T(8,128)(2,1)}, u32[]{:S(2)}, u32[]{:S(2)}) collective-permute-start(bf16[48,4096]{1,0:T(8,128)(2,1)} %collective-permute-done.14.refs_4_), channel_id=1, source_target_pairs={{0,1},{1,0},{2,3},{3,2},{4,5},{5,4},{6,7},{7,6},{8,9},{9,8},{10,11... | collective-permute-start | bytes 1179656 | tf_op jit(solution)/shard_map/ppermute | solution.py:175
  101.1 2.6 %shard_map.175.hid_ref = bf16[288,112]{1,0:T(8,128)(2,1)S(1)} custom-call(s32[1]{0:T(128)} %bitcast.core_ref, bf16[4,2,112,1024]{3,2,1,0:T(8,128)(2,1)S(1)} %get-tuple-element.8.w_ref, bf16[96,4096]{1,0:T(8,128)(2,1)} %constant_dynamic-update-slice_fusion.refs_0_, bf16[96,4096]{1,0:T(8,128)(2,1)S(1)} %collective-permute-done.8.refs_1_, ...), custom_call_target="tpu_custom_call" | custom-call | flops 530000000 | bytes 6500000 | tf_op jit(solution)/shard_map/pallas_call | solution.py:180
  103.8 4.4 %shard_map.176 = (f32[112,4096]{1,0:T(8,128)}, f32[1,112]{1,0:T(1,128)}) custom-call(s32[1]{0:T(128)} %bitcast.core_ref, s32[1,384]{1,0:T(1,128)S(1)} %broadcast_in_dim.14.idt_ref, s32[384,1]{1,0:T(8,128)S(1)} %broadcast_in_dim.17.idc_ref, bf16[288,112]{1,0:T(8,128)(2,1)S(1)} %shard_map.175.hid_ref, bf16[4,2,112,1024]{3,2,1,0:T(8,128)(2,1)S(1)} %get-tuple-element.8.w_ref, ...), custom_call_target="tpu_custom_call" | custom-call | flops 530000000 | bytes 9000000 | tf_op jit(solution)/shard_map/pallas_call | solution.py:189
  (54 shorter events, 3.5 us)
Async XLA Ops:
  7.2 30.3 %copy-start.3 = (f32[32768]{0:T(1024)S(1)}, f32[32768]{0:T(1024)}, u32[]{:S(2)}) copy-start(f32[32768]{0:T(1024)} %param.21) | copy-start | bytes 393220
  7.2 30.3 %copy-start.4 = (f32[32768]{0:T(1024)S(1)}, f32[32768]{0:T(1024)}, u32[]{:S(2)}) copy-start(f32[32768]{0:T(1024)} %param.23) | copy-start | bytes 393220
  7.2 77.9 %all-gather.3.cloned.1.call-start = ((), (), s32[]{:S(2)}) async-start(), calls=%async_computation | async-start | bytes 2293760 | tf_op jit(solution)/shard_map/all_gather | solution.py:147
  8.2 11.8 %collective-permute-start = (bf16[96,128]{1,0:T(8,128)(2,1)S(1)}, bf16[96,128]{1,0:T(8,128)(2,1)S(1)}, u32[]{:S(2)}, u32[]{:S(2)}) collective-permute-start(bf16[96,128]{1,0:T(8,128)(2,1)S(1)} %select_n.53), channel_id=1, source_target_pairs={{0,1},{1,0},{2,3},{3,2},{4,5},{5,4},{6,7},{7,6},{8,9},{9,8},{10,11... | collective-permute-start | bytes 73736 | tf_op jit(solution)/shard_map/ppermute | solution.py:151
  17.9 7.0 %collective-permute-start.3 = (f32[32768]{0:T(1024)S(1)}, f32[32768]{0:T(1024)S(1)}, u32[]{:S(2)}, u32[]{:S(2)}) collective-permute-start(f32[32768]{0:T(1024)S(1)} %sub.27), channel_id=1, source_target_pairs={{0,128},{128,0},{256,384},{384,256},{1,129},{129,1},{257,385},{385... | collective-permute-start | bytes 393224 | tf_op jit(solution)/shard_map/ppermute | solution.py:154
  19.9 9.2 %collective-permute-start.1 = (bf16[192,128]{1,0:T(8,128)(2,1)S(1)}, bf16[192,128]{1,0:T(8,128)(2,1)S(1)}, u32[]{:S(2)}, u32[]{:S(2)}) collective-permute-start(bf16[192,128]{1,0:T(8,128)(2,1)S(1)} %pad_maximum_fusion.2), channel_id=1, source_target_pairs={{0,2},{1,3},{2,0},{3,1},{4,6},{5,7},{6,4},{7,5},{8,10},{9,11},{10,... | collective-permute-start | bytes 147464 | tf_op jit(solution)/shard_map/ppermute | solution.py:156
  25.0 12.5 %collective-permute-start.4 = (f32[32768]{0:T(1024)S(1)}, f32[32768]{0:T(1024)S(1)}, u32[]{:S(2)}, u32[]{:S(2)}) collective-permute-start(f32[32768]{0:T(1024)S(1)} %add.102), channel_id=1, source_target_pairs={{0,256},{256,0},{128,384},{384,128},{1,257},{257,1},{129,385},{385... | collective-permute-start | bytes 393224 | tf_op jit(solution)/shard_map/ppermute | solution.py:155
  29.1 10.4 %collective-permute-start.2 = (bf16[384,128]{1,0:T(8,128)(2,1)S(1)}, bf16[384,128]{1,0:T(8,128)(2,1)S(1)}, u32[]{:S(2)}, u32[]{:S(2)}) collective-permute-start(bf16[384,128]{1,0:T(8,128)(2,1)S(1)} %pad_maximum_fusion.1), channel_id=1, source_target_pairs={{0,16},{1,17},{2,18},{3,19},{4,20},{5,21},{6,22},{7,23},{8,24},{9,... | collective-permute-start | bytes 294920 | tf_op jit(solution)/shard_map/ppermute | solution.py:157
  39.7 21.6 %collective-permute-start.7 = (bf16[24,4096]{1,0:T(8,128)(2,1)S(1)}, bf16[24,4096]{1,0:T(8,128)(2,1)S(1)}, u32[]{:S(2)}, u32[]{:S(2)}) collective-permute-start(bf16[24,4096]{1,0:T(8,128)(2,1)S(1)} %add.106), channel_id=1, source_target_pairs={{0,64},{1,25},{2,66},{3,27},{4,68},{5,29},{6,70},{7,31},{8,72},{9,... | collective-permute-start | bytes 589832 | tf_op jit(solution)/shard_map/ppermute | solution.py:159
  49.9 10.7 %collective-permute-start.6 = (bf16[24,4096]{1,0:T(8,128)(2,1)S(1)}, bf16[24,4096]{1,0:T(8,128)(2,1)S(1)}, u32[]{:S(2)}, u32[]{:S(2)}) collective-permute-start(bf16[24,4096]{1,0:T(8,128)(2,1)S(1)} %add.106), channel_id=1, source_target_pairs={{0,96},{1,29},{2,98},{3,31},{4,100},{5,1},{6,102},{7,3},{8,104},{9... | collective-permute-start | bytes 589832 | tf_op jit(solution)/shard_map/ppermute | solution.py:159
  51.8 8.0 %collective-permute-start.5 = (bf16[24,4096]{1,0:T(8,128)(2,1)S(1)}, bf16[24,4096]{1,0:T(8,128)(2,1)S(1)}, u32[]{:S(2)}, u32[]{:S(2)}) collective-permute-start(bf16[24,4096]{1,0:T(8,128)(2,1)S(1)} %add.106), channel_id=1, source_target_pairs={{0,32},{1,5},{2,34},{3,7},{4,36},{5,9},{6,38},{7,11},{8,40},{9,13}... | collective-permute-start | bytes 589832 | tf_op jit(solution)/shard_map/ppermute | solution.py:159
  61.9 38.9 %copy-start.5 = (s32[384]{0:T(512)S(1)}, s32[384]{0:T(512)}, u32[]{:S(2)}) copy-start(s32[384]{0:T(512)} %constant.105) | copy-start | bytes 4612
  61.9 38.9 %copy-start.6 = (s32[384]{0:T(512)S(1)}, s32[384]{0:T(512)}, u32[]{:S(2)}) copy-start(s32[384]{0:T(512)} %constant.96.clone) | copy-start | bytes 4612
  61.9 39.0 %copy-start.7 = (s32[384]{0:T(512)S(1)}, s32[384]{0:T(512)}, u32[]{:S(2)}) copy-start(s32[384]{0:T(512)} %constant.95.clone) | copy-start | bytes 4612
  61.9 39.0 %copy-start.8 = (s32[384]{0:T(512)S(1)}, s32[384]{0:T(512)}, u32[]{:S(2)}) copy-start(s32[384]{0:T(512)} %constant.94.clone) | copy-start | bytes 4612
  61.9 39.0 %copy-start.9 = (s32[384]{0:T(512)S(1)}, s32[384]{0:T(512)}, u32[]{:S(2)}) copy-start(s32[384]{0:T(512)} %constant.93.clone) | copy-start | bytes 4612
  61.9 39.0 %copy-start.10 = (s32[384]{0:T(512)S(1)}, s32[384]{0:T(512)}, u32[]{:S(2)}) copy-start(s32[384]{0:T(512)} %constant.92.clone) | copy-start | bytes 4612
  61.9 39.0 %copy-start.11 = (s32[384]{0:T(512)S(1)}, s32[384]{0:T(512)}, u32[]{:S(2)}) copy-start(s32[384]{0:T(512)} %constant.91.clone) | copy-start | bytes 4612
  61.9 14.7 %collective-permute-start.8 = (bf16[96,4096]{1,0:T(8,128)(2,1)}, bf16[96,4096]{1,0:T(8,128)(2,1)S(1)}, u32[]{:S(2)}, u32[]{:S(2)}) collective-permute-start(bf16[96,4096]{1,0:T(8,128)(2,1)} %constant_dynamic-update-slice_fusion.refs_0_), channel_id=1, source_target_pairs={{0,4},{1,33},{2,6},{3,35},{4,8},{5,37},{6,10},{7,39},{8,12},{9,41}... | collective-permute-start | bytes 2359304 | tf_op jit(solution)/shard_map/ppermute | solution.py:172
  65.0 18.1 %collective-permute-start.9 = (bf16[96,4096]{1,0:T(8,128)(2,1)}, bf16[96,4096]{1,0:T(8,128)(2,1)S(1)}, u32[]{:S(2)}, u32[]{:S(2)}) collective-permute-start(bf16[96,4096]{1,0:T(8,128)(2,1)} %constant_dynamic-update-slice_fusion.refs_0_), channel_id=1, source_target_pairs={{0,28},{1,97},{2,30},{3,99},{4,0},{5,101},{6,2},{7,103},{8,4},{9,1... | collective-permute-start | bytes 2359304 | tf_op jit(solution)/shard_map/ppermute | solution.py:172
  68.6 32.5 %collective-permute-start.10 = (bf16[96,4096]{1,0:T(8,128)(2,1)}, bf16[96,4096]{1,0:T(8,128)(2,1)}, u32[]{:S(2)}, u32[]{:S(2)}) collective-permute-start(bf16[96,4096]{1,0:T(8,128)(2,1)} %constant_dynamic-update-slice_fusion.refs_0_), channel_id=1, source_target_pairs={{0,1},{1,0},{2,3},{3,2},{4,5},{5,4},{6,7},{7,6},{8,9},{9,8},{10,11... | collective-permute-start | bytes 2359304 | tf_op jit(solution)/shard_map/ppermute | solution.py:175
  77.4 13.7 %collective-permute-start.13 = (bf16[48,4096]{1,0:T(8,128)(2,1)}, bf16[48,4096]{1,0:T(8,128)(2,1)}, u32[]{:S(2)}, u32[]{:S(2)}) collective-permute-start(bf16[48,4096]{1,0:T(8,128)(2,1)} %slice.17), channel_id=1, source_target_pairs={{0,4},{1,33},{2,6},{3,35},{4,8},{5,37},{6,10},{7,39},{8,12},{9,41}... | collective-permute-start | bytes 1179656 | tf_op jit(solution)/shard_map/ppermute | solution.py:173
  79.3 21.7 %collective-permute-start.11 = (bf16[96,4096]{1,0:T(8,128)(2,1)S(1)}, bf16[96,4096]{1,0:T(8,128)(2,1)}, u32[]{:S(2)}, u32[]{:S(2)}) collective-permute-start(bf16[96,4096]{1,0:T(8,128)(2,1)S(1)} %collective-permute-done.8.refs_1_), channel_id=1, source_target_pairs={{0,1},{1,0},{2,3},{3,2},{4,5},{5,4},{6,7},{7,6},{8,9},{9,8},{10,11... | collective-permute-start | bytes 2359304 | tf_op jit(solution)/shard_map/ppermute | solution.py:175
  83.2 17.9 %collective-permute-start.12 = (bf16[96,4096]{1,0:T(8,128)(2,1)S(1)}, bf16[96,4096]{1,0:T(8,128)(2,1)}, u32[]{:S(2)}, u32[]{:S(2)}) collective-permute-start(bf16[96,4096]{1,0:T(8,128)(2,1)S(1)} %collective-permute-done.9.refs_2_), channel_id=1, source_target_pairs={{0,1},{1,0},{2,3},{3,2},{4,5},{5,4},{6,7},{7,6},{8,9},{9,8},{10,11... | collective-permute-start | bytes 2359304 | tf_op jit(solution)/shard_map/ppermute | solution.py:175
  85.1 1.5 %copy-start.1 = (bf16[8,112,1024]{2,1,0:T(8,128)(2,1)S(1)}, bf16[8,112,1024]{2,1,0:T(8,128)(2,1)}, u32[]{:S(2)}) copy-start(bf16[8,112,1024]{2,1,0:T(8,128)(2,1)} %all-gather.3.cloned.1.call-done) | copy-start | bytes 5505028
  88.0 8.9 %collective-permute-start.14 = (bf16[48,4096]{1,0:T(8,128)(2,1)S(1)}, bf16[48,4096]{1,0:T(8,128)(2,1)}, u32[]{:S(2)}, u32[]{:S(2)}) collective-permute-start(bf16[48,4096]{1,0:T(8,128)(2,1)S(1)} %slice_add_fusion), channel_id=1, source_target_pairs={{0,28},{1,97},{2,30},{3,99},{4,0},{5,101},{6,2},{7,103},{8,4},{9,1... | collective-permute-start | bytes 1179656 | tf_op jit(solution)/shard_map/ppermute | solution.py:173
  91.1 12.6 %collective-permute-start.15 = (bf16[48,4096]{1,0:T(8,128)(2,1)}, bf16[48,4096]{1,0:T(8,128)(2,1)}, u32[]{:S(2)}, u32[]{:S(2)}) collective-permute-start(bf16[48,4096]{1,0:T(8,128)(2,1)} %collective-permute-done.13.refs_3_), channel_id=1, source_target_pairs={{0,1},{1,0},{2,3},{3,2},{4,5},{5,4},{6,7},{7,6},{8,9},{9,8},{10,11... | collective-permute-start | bytes 1179656 | tf_op jit(solution)/shard_map/ppermute | solution.py:175
  96.9 6.9 %collective-permute-start.16 = (bf16[48,4096]{1,0:T(8,128)(2,1)}, bf16[48,4096]{1,0:T(8,128)(2,1)}, u32[]{:S(2)}, u32[]{:S(2)}) collective-permute-start(bf16[48,4096]{1,0:T(8,128)(2,1)} %collective-permute-done.14.refs_4_), channel_id=1, source_target_pairs={{0,1},{1,0},{2,3},{3,2},{4,5},{5,4},{6,7},{7,6},{8,9},{9,8},{10,11... | collective-permute-start | bytes 1179656 | tf_op jit(solution)/shard_map/ppermute | solution.py:175
  101.1 2.7 %copy-start = (f32[1,112,4096]{2,1,0:T(8,128)S(1)}, f32[1,112,4096]{2,1,0:T(8,128)}, u32[]{:S(2)}) copy-start(f32[1,112,4096]{2,1,0:T(8,128)} %param.19) | copy-start | bytes 5505028
  101.1 2.7 %copy-start.2 = (f32[1,112]{1,0:T(1,128)S(1)}, f32[1,112]{1,0:T(1,128)}, u32[]{:S(2)}) copy-start(f32[1,112]{1,0:T(1,128)} %sm_ref.1) | copy-start | bytes 1348
Sparse Core Ops, SparseCore 0:
  28.9 48.4 all-gather.2
